TPU v7x, 512 devices: a whole 4x4x16 slice. The times are simulated.
512 devices in a mesh: dom: 64 (over z, x), elem: 8 (over y, core).
Axes of the slice: x: 4, y: 4, z: 16, core: 2. Of those that a mesh axis runs over, the one named last changes fastest.
Arguments:
- adjoint: float32 [4, 125, 131072], P(None, None, ('dom', 'elem')), may hold values from -6 to 6
- adjoint_reg: float32 [4, 125, 131072], P(None, None, ('dom', 'elem')), may hold values from -4 to 4
- metric: float32 [3, 131072], P(None, ('dom', 'elem')), may hold values from 1 to 4
- face_link: int32 [6, 131072], P(None, ('dom', 'elem')), may hold values from -1 to 2815, as said below
- orient: int32 [6, 131072], P(None, ('dom', 'elem')), may hold values from 0 to 7
- intra_send: int32 [65536], P(('dom', 'elem')), may hold values from 0 to 1535
- part_send: int32 [4, 32768], P(None, ('dom', 'elem')), may hold values from 0 to 1535
- wall_face: int32 [65536], P(('dom', 'elem')), may hold values from -1 to 1535, as said below
- wall_patch: int32 [65536], P(('dom', 'elem')), may hold values from 0 to 4095
- pole_count: int32 [4096], replicated, may hold values from 1 to 6
- amplitude: float32 [4096, 6], replicated, may hold values from -4 to 4
- pole_decay: float32 [4096, 6], replicated, may hold values from 0.5 to 10
- wall_aux: float32 [6, 25, 65536], P(None, None, ('dom', 'elem')), may hold values from -6 to 6
- wall_aux_reg: float32 [6, 25, 65536], P(None, None, ('dom', 'elem')), may hold values from -4 to 4
- forward_aux: bfloat16 [2, 6, 25, 65536], P(None, None, None, ('dom', 'elem')), may hold values from -6 to 6
Outputs:
- adjoint_out: float32 [4, 125, 131072], P(None, None, ('dom', 'elem'))
- adjoint_reg_out: float32 [4, 125, 131072], P(None, None, ('dom', 'elem'))
- wall_aux_out: float32 [6, 25, 65536], P(None, None, ('dom', 'elem'))
- wall_aux_reg_out: float32 [6, 25, 65536], P(None, None, ('dom', 'elem'))
- patch_grad: float32 [4096, 6], P(('dom', 'elem'))
Inputs may be any that keep to these rules, and one draw needn't show every extreme that they name: `face_link`: -1 marks a wall face; on each device the faces marked -1 are exactly those listed in its block of wall_face. `wall_face`: each device's block lists distinct faces first and -1 in the remaining slots; at most 128 wall faces a device, and some device has all 128 slots filled.
All inputs are finite; a program needn't handle non-finite values.
Results may differ from a plain program's by a relative error of at most 0.00035.
Values sent between devices are 32-bit elements; how exact they have to be, the bound alone decides.
A program may use at most 64 MiB of HBM per device.

v0:
```python
import jax
import jax.numpy as jnp
import numpy as np
from jax import lax
from jax.sharding import PartitionSpec as P

DT_STEP = 0.1
SECTION_A = (-1.514183444257, -1.697784692471)
SECTION_B = (0.1530572479681, 0.6994504559488)
OFFSETS = (-2, -1, 1, 2)
PRECISE = lax.Precision.HIGHEST


def shifted(shard, axis, by):
    length = lax.axis_size(axis)
    return lax.ppermute(shard, axis, [(i, (i + by) % length) for i in range(length)])


def lobatto_tables():
    node_points = np.array([-1.0, -np.sqrt(3.0 / 7.0), 0.0, np.sqrt(3.0 / 7.0), 1.0])
    quad_line = np.array([0.1, 49.0 / 90.0, 32.0 / 45.0, 49.0 / 90.0, 0.1])
    bary_weight = np.array(
        [
            1.0 / np.prod([node_points[j] - node_points[k] for k in range(5) if k != j])
            for j in range(5)
        ]
    )
    line_deriv = np.zeros((5, 5))
    for i in range(5):
        for j in range(5):
            if i != j:
                line_deriv[i, j] = (
                    bary_weight[j] / bary_weight[i] / (node_points[i] - node_points[j])
                )
        line_deriv[i, i] = -np.sum(line_deriv[i])
    return (line_deriv, quad_line)


def dense_tables():
    line_deriv, quad_line = lobatto_tables()
    identity = np.eye(5)
    along_axes = [
        np.kron(np.kron(line_deriv, identity), identity),
        np.kron(np.kron(identity, line_deriv), identity),
        np.kron(np.kron(identity, identity), line_deriv),
    ]
    return (
        jnp.asarray(np.concatenate(along_axes, 0), jnp.float32),
        jnp.asarray(np.concatenate(along_axes, 1), jnp.float32),
    )


def face_traces(node_grid):
    face_list = [
        node_grid[:, 0],
        node_grid[:, 4],
        node_grid[:, :, 0],
        node_grid[:, :, 4],
        node_grid[:, :, :, 0],
        node_grid[:, :, :, 4],
    ]
    return jnp.stack(face_list, axis=3)


def orient_faces(gathered, orient_flat):
    result = gathered
    for symmetry in range(1, 8):
        variant = gathered
        if symmetry & 4:
            variant = jnp.swapaxes(variant, 1, 2)
        if symmetry & 1:
            variant = variant[:, ::-1]
        if symmetry & 2:
            variant = variant[:, :, ::-1]
        result = jnp.where(orient_flat == symmetry, variant, result)
    return result


def volume_dense(adjoint_now, metric_dev):
    stack_table, concat_table = dense_tables()
    elements = adjoint_now.shape[-1]
    grads = jnp.dot(
        stack_table, adjoint_now[0], precision=PRECISE, preferred_element_type=jnp.float32
    )
    grads = grads.reshape(3, 125, elements) * metric_dev[:, None, :]
    scaled = (adjoint_now[1:4] * metric_dev[:, None, :]).reshape(375, elements)
    diverge = jnp.dot(concat_table, scaled, precision=PRECISE, preferred_element_type=jnp.float32)
    return jnp.concatenate([-diverge[None], -grads], axis=0)


def lift_faces(residual, face_flux, metric_dev):
    elements = residual.shape[-1]
    grid_residual = residual.reshape(4, 5, 5, 5, elements)
    for face_id in range(6):
        axis_id = face_id // 2
        edge_node = 0 if face_id % 2 == 0 else 4
        normal_sign = -1.0 if face_id % 2 == 0 else 1.0
        lifted = 10.0 * metric_dev[axis_id] * face_flux[:, :, face_id]
        position = (slice(None),) * axis_id + (edge_node,)
        grid_residual = grid_residual.at[(0,) + position].add(lifted)
        grid_residual = grid_residual.at[(1 + axis_id,) + position].add(-normal_sign * lifted)
    return grid_residual.reshape(4, 125, elements)


def section_update(
    adjoint_now,
    register,
    trace_grid,
    trace_pool,
    metric_dev,
    link_dev,
    orient_dev,
    wall_dev,
    patch_dev,
    pole_count,
    amplitude,
    pole_decay,
    aux_state,
    aux_reg,
    forward_dev,
    section_id,
    volume,
):
    elements = adjoint_now.shape[-1]
    face_count = 6 * elements
    coef_a = SECTION_A[section_id]
    coef_b = SECTION_B[section_id]
    link_flat = link_dev.reshape(-1)
    is_wall = link_flat < 0
    near_trace = jnp.take(trace_pool, jnp.where(is_wall, 0, link_flat), axis=1).reshape(
        4, 5, 5, face_count
    )
    near_trace = orient_faces(near_trace, orient_dev.reshape(-1))
    own_trace = trace_grid.reshape(4, 5, 5, face_count)
    face_of = jnp.arange(face_count, dtype=jnp.int32) // elements
    axis_of = face_of // 2
    sign_of = jnp.where(face_of % 2 == 0, -1.0, 1.0).astype(jnp.float32)

    def normal_part(face_grid):
        return sign_of * jnp.where(
            axis_of == 0, face_grid[1], jnp.where(axis_of == 1, face_grid[2], face_grid[3])
        )

    un_own = normal_part(own_trace).reshape(25, face_count)
    un_near = normal_part(near_trace).reshape(25, face_count)
    live_slot = wall_dev >= 0
    un_slot = jnp.take(un_own, jnp.where(live_slot, wall_dev, 0), axis=1) * live_slot.astype(
        jnp.float32
    )
    pole_total = amplitude.shape[1]
    active = (
        (
            jnp.arange(pole_total, dtype=jnp.int32)[:, None]
            < jnp.take(pole_count, patch_dev)[None, :]
        )
        & live_slot[None, :]
    ).astype(jnp.float32)
    amp_slot = jnp.take(amplitude, patch_dev, axis=0).T
    decay_slot = jnp.take(pole_decay, patch_dev, axis=0).T
    wall_value = jnp.sum((active * amp_slot)[:, None, :] * aux_state, axis=0)
    wall_face_value = (
        jnp.zeros((25, face_count), jnp.float32)
        .at[:, jnp.where(live_slot, wall_dev, face_count)]
        .set(wall_value, mode="drop")
    )
    jump_p = jnp.where(is_wall, 0.0, (near_trace[0] - own_trace[0]).reshape(25, face_count))
    jump_un = jnp.where(is_wall, 2.0 * wall_face_value - 2.0 * un_own, un_near - un_own)
    face_flux = (0.5 * (jump_p - jump_un)).reshape(5, 5, 6, elements)
    residual = lift_faces(volume(adjoint_now, metric_dev), face_flux, metric_dev)
    register = coef_a * register + DT_STEP * residual
    adjoint_now = adjoint_now + coef_b * register
    aux_rate = active[:, None, :] * (un_slot[None] - decay_slot[:, None, :] * aux_state)
    aux_reg = coef_a * aux_reg + DT_STEP * aux_rate
    aux_state = aux_state + coef_b * aux_reg
    line_deriv, quad_line = lobatto_tables()
    quad_weight = jnp.asarray(np.outer(quad_line, quad_line).reshape(25), jnp.float32)
    grad_term = (
        coef_b
        * DT_STEP
        * active
        * jnp.sum(quad_weight[None, :, None] * un_slot[None] * forward_dev, axis=1)
    )
    partial_value = jax.ops.segment_sum(grad_term.T, patch_dev, num_segments=amplitude.shape[0])
    return (adjoint_now, register, aux_state, aux_reg, partial_value)


def body(
    adjoint,
    adjoint_reg,
    metric,
    face_link,
    orient,
    intra_send,
    part_send,
    wall_face,
    wall_patch,
    pole_count,
    amplitude,
    pole_decay,
    wall_aux,
    wall_aux_reg,
    forward_aux,
):
    elements = adjoint.shape[-1]
    adjoint_now, register, aux_state, aux_reg = (adjoint, adjoint_reg, wall_aux, wall_aux_reg)
    grad_total = jnp.zeros(amplitude.shape, jnp.float32)
    for section_id in range(forward_aux.shape[0]):
        trace_grid = face_traces(adjoint_now.reshape(4, 5, 5, 5, elements))
        flat_traces = trace_grid.reshape(100, 6 * elements)
        intra_pool = lax.all_gather(
            jnp.take(flat_traces, intra_send, axis=1), "elem", axis=1, tiled=True
        )
        outward = jnp.take(flat_traces, part_send, axis=1)
        received = [
            shifted(outward[:, slot_id], "dom", offset) for slot_id, offset in enumerate(OFFSETS)
        ]
        trace_pool = jnp.concatenate([flat_traces, intra_pool] + received, axis=1)
        adjoint_now, register, aux_state, aux_reg, partial_value = section_update(
            adjoint_now,
            register,
            trace_grid,
            trace_pool,
            metric,
            face_link,
            orient,
            wall_face,
            wall_patch,
            pole_count,
            amplitude,
            pole_decay,
            aux_state,
            aux_reg,
            forward_aux[section_id].astype(jnp.float32),
            section_id,
            volume_dense,
        )
        grad_total = grad_total + lax.psum(partial_value, ("dom", "elem"))
    share = amplitude.shape[0] // lax.axis_size(("dom", "elem"))
    patch_grad = lax.dynamic_slice_in_dim(
        grad_total, lax.axis_index(("dom", "elem")) * share, share, 0
    )
    return (adjoint_now, register, aux_state, aux_reg, patch_grad)


def solution(mesh):
    in_specs = (
        P(None, None, ("dom", "elem")),
        P(None, None, ("dom", "elem")),
        P(None, ("dom", "elem")),
        P(None, ("dom", "elem")),
        P(None, ("dom", "elem")),
        P(("dom", "elem")),
        P(None, ("dom", "elem")),
        P(("dom", "elem")),
        P(("dom", "elem")),
        P(),
        P(),
        P(),
        P(None, None, ("dom", "elem")),
        P(None, None, ("dom", "elem")),
        P(None, None, None, ("dom", "elem")),
    )
    out_specs = (
        P(None, None, ("dom", "elem")),
        P(None, None, ("dom", "elem")),
        P(None, None, ("dom", "elem")),
        P(None, None, ("dom", "elem")),
        P(("dom", "elem"), None),
    )
    return jax.shard_map(body, mesh=mesh, in_specs=in_specs, out_specs=out_specs, check_vma=False)
```

profile of v0, /device:TPU:1, one launch (start us, length us, event | category | flops | bytes accessed | tf_op | source)
XLA Modules:
  0.0 693.4 jit_solution(4211417787595429243)
XLA Ops:
  15.4 14.4 %collective-permute-start = (f32[100,64]{0,1:T(8,128)}, f32[100,64]{0,1:T(8,128)}, u32[]{:S(2)}, u32[]{:S(2)}) collective-permute-start(f32[100,64]{0,1:T(8,128)} %get-tuple-element.372), channel_id=1, source_target_pairs={{0,496},{8,504},{16,0},{24,8},{32,16},{40,24},{48,32},{56,40},{64,... | collective-permute-start | bytes 76808 | tf_op jit(solution)/shard_map/ppermute | solution.py:16
  29.8 2.8 collective-permute-start.1
  32.6 2.5 collective-permute-start.2
  35.1 2.6 collective-permute-start.3
  41.4 2.1 concatenate.82
  43.5 2.0 concatenate.83
  47.5 16.1 %all_gather.6 = f32[100,1024]{0,1:T(8,128)} all-gather(f32[100,128]{0,1:T(8,128)S(1)} %select_bitcast_fusion.6), channel_id=1, replica_groups=mesh['dom'=64,'elem'=8] {'elem'}, dimensions={1}, use_global_device_ids=true | all-gather | bytes 460800 | tf_op jit(solution)/shard_map/all_gather | solution.py:210
  67.5 1.5 copy.225
  69.0 1.4 gather_fusion.4
  71.6 1.6 copy.249
  73.2 1.4 gather_fusion.9
  77.3 1.4 fusion
  82.9 1.4 scatter_custom_fusion
  91.4 2.6 gather_fusion.2
  95.0 4.2 rev.40
  99.2 4.1 rev.41
  103.4 4.1 rev.43
  107.5 4.2 rev.44
  111.7 2.7 fusion.12
  115.9 1.9 fusion.32
  117.9 2.0 fusion.33
  120.5 2.0 broadcast_select_fusion.1
  122.5 1.5 scatter-add.110
  127.6 1.4 gather_fusion.5
  129.0 1.3 gather_fusion.6
  130.4 4.5 slice_reduce_fusion.3
  135.0 14.2 %all_gather.7 = f32[100,1024]{0,1:T(8,128)} all-gather(f32[100,128]{0,1:T(8,128)S(1)} %select_bitcast_fusion.5), channel_id=1, replica_groups=mesh['dom'=64,'elem'=8] {'elem'}, dimensions={1}, use_global_device_ids=true | all-gather | bytes 460800 | tf_op jit(solution)/shard_map/all_gather | solution.py:210
  150.0 6.6 collective-permute-start.4
  156.6 4.0 collective-permute-start.5
  160.6 1.9 collective-permute-start.6
  162.5 1.9 collective-permute-start.7
  167.7 1.4 fusion.1
  176.7 2.6 gather_fusion.7
  180.4 4.2 rev.46
  184.6 4.1 rev.47
  188.7 4.1 rev.49
  192.9 4.2 rev.50
  197.1 2.7 fusion.18
  202.0 1.2 copy.260
  205.2 1.6 scatter_custom_fusion.2
  207.0 2.6 scatter_custom_fusion.3
  209.6 3.1 add.307
  214.0 1.9 fusion.34
  216.0 2.0 fusion.35
  218.4 2.0 broadcast_select_fusion
  220.5 1.5 scatter-add.156
  227.1 458.2 %all-reduce.2.cloned.1.call-done = f32[4096,6]{1,0:T(8,128)} async-done(((f32[4096,6]{1,0:T(8,128)}), f32[4096,6]{1,0:T(8,128)}) %all-reduce.2.cloned.1.call-update) | async-done | bytes 98320 | tf_op jit(solution)/shard_map/psum | solution.py:237
  685.3 1.3 constant_dynamic-slice_fusion
  (397 shorter events, 62.2 us)
Async XLA Ops:
  7.2 59.1 %copy-start = (s32[4096]{0:T(1024)S(1)}, s32[4096]{0:T(1024)}, u32[]{:S(2)}) copy-start(s32[4096]{0:T(1024)} %param.90) | copy-start | bytes 49156
  7.2 678.1 %all-reduce.2.cloned.1.call-start = ((), (), s32[]{:S(2)}) async-start(), calls=%async_computation | async-start | bytes 4194304 | tf_op jit(solution)/shard_map/psum | solution.py:237
  11.5 3.1 copy-start.84
  14.6 23.1 %copy-start.68 = (s32[6,256]{1,0:T(8,128)S(1)}, s32[6,256]{1,0:T(8,128)}, u32[]{:S(2)}) copy-start(s32[6,256]{1,0:T(8,128)} %param.84) | copy-start | bytes 18436
  15.4 72.9 %collective-permute-start = (f32[100,64]{0,1:T(8,128)}, f32[100,64]{0,1:T(8,128)}, u32[]{:S(2)}, u32[]{:S(2)}) collective-permute-start(f32[100,64]{0,1:T(8,128)} %get-tuple-element.372), channel_id=1, source_target_pairs={{0,496},{8,504},{16,0},{24,8},{32,16},{40,24},{48,32},{56,40},{64,... | collective-permute-start | bytes 76808 | tf_op jit(solution)/shard_map/ppermute | solution.py:16
  29.8 59.3 %collective-permute-start.1 = (f32[100,64]{0,1:T(8,128)}, f32[100,64]{0,1:T(8,128)}, u32[]{:S(2)}, u32[]{:S(2)}) collective-permute-start(f32[100,64]{0,1:T(8,128)} %get-tuple-element.371), channel_id=1, source_target_pairs={{0,504},{8,0},{16,8},{24,16},{32,24},{40,32},{48,40},{56,48},{64,5... | collective-permute-start | bytes 76808 | tf_op jit(solution)/shard_map/ppermute | solution.py:16
  32.6 57.2 %collective-permute-start.2 = (f32[100,64]{0,1:T(8,128)}, f32[100,64]{0,1:T(8,128)}, u32[]{:S(2)}, u32[]{:S(2)}) collective-permute-start(f32[100,64]{0,1:T(8,128)} %get-tuple-element.370), channel_id=1, source_target_pairs={{0,8},{8,16},{16,24},{24,32},{32,40},{40,48},{48,56},{56,64},{64,7... | collective-permute-start | bytes 76808 | tf_op jit(solution)/shard_map/ppermute | solution.py:16
  35.1 55.5 %collective-permute-start.3 = (f32[100,64]{0,1:T(8,128)}, f32[100,64]{0,1:T(8,128)}, u32[]{:S(2)}, u32[]{:S(2)}) collective-permute-start(f32[100,64]{0,1:T(8,128)} %get-tuple-element.369), channel_id=1, source_target_pairs={{0,16},{8,24},{16,32},{24,40},{32,48},{40,56},{48,64},{56,72},{64,... | collective-permute-start | bytes 76808 | tf_op jit(solution)/shard_map/ppermute | solution.py:16
  37.7 7.8 %copy-start.96 = (s32[128]{0:T(128)S(1)}, s32[128]{0:T(128)}, u32[]{:S(2)}) copy-start(s32[128]{0:T(128)} %param.88) | copy-start | bytes 1540
  37.7 8.4 %copy-start.92 = (s32[128]{0:T(128)S(1)}, s32[128]{0:T(128)}, u32[]{:S(2)}) copy-start(s32[128]{0:T(128)} %param.86) | copy-start | bytes 1540
  37.8 9.0 %copy-start.93 = (s32[128]{0:T(128)S(1)}, s32[128]{0:T(128)}, u32[]{:S(2)}) copy-start(s32[128]{0:T(128)} %param.89) | copy-start | bytes 1540
  39.8 23.8 %copy-start.69 = (s32[6,256]{1,0:T(8,128)S(1)}, s32[6,256]{1,0:T(8,128)}, u32[]{:S(2)}) copy-start(s32[6,256]{1,0:T(8,128)} %param.85) | copy-start | bytes 18436
  39.8 24.4 %copy-start.14 = (f32[1,5,5,6,256]{4,3,2,1,0:T(8,128)S(1)}, f32[1,5,5,6,256]{4,3,2,1,0:T(8,128)}, u32[]{:S(2)}) copy-start(f32[1,5,5,6,256]{4,3,2,1,0:T(8,128)} %get-tuple-element.350) | copy-start | bytes 460804
  39.8 24.7 %copy-start.42 = (pred[1536]{0:T(1024)(128)(4,1)}, pred[1536]{0:T(1024)(128)(4,1)S(1)}, u32[]{:S(2)}) copy-start(pred[1536]{0:T(1024)(128)(4,1)S(1)} %get-tuple-element.397) | copy-start | bytes 4612
  39.8 24.7 %copy-start.44 = (pred[1536]{0:T(1024)(128)(4,1)}, pred[1536]{0:T(1024)(128)(4,1)S(1)}, u32[]{:S(2)}) copy-start(pred[1536]{0:T(1024)(128)(4,1)S(1)} %get-tuple-element.398) | copy-start | bytes 4612
  39.9 24.7 %copy-start.36 = (f32[1536]{0:T(1024)}, f32[1536]{0:T(1024)S(1)}, u32[]{:S(2)}) copy-start(f32[1536]{0:T(1024)S(1)} %fusion.72) | copy-start | bytes 18436
  40.8 6.0 copy-start.88
  46.7 17.7 %copy-start.86 = (pred[128]{0:T(512)(128)(4,1)}, pred[128]{0:T(512)(128)(4,1)S(1)}, u32[]{:S(2)}) copy-start(pred[128]{0:T(512)(128)(4,1)S(1)} %get-tuple-element.401) | copy-start | bytes 388
  67.5 3.0 copy-start.66
  71.6 10.3 %copy-start.40 = (f32[6,128]{1,0:T(8,128)}, f32[6,128]{1,0:T(8,128)S(1)}, u32[]{:S(2)}) copy-start(f32[6,128]{1,0:T(8,128)S(1)} %copy.246) | copy-start | bytes 9220
  71.6 4.0 copy-start.38
  76.8 3.4 copy-start.6
  80.5 4.8 copy-start.13
  82.1 29.6 %copy-start.47 = (pred[1536]{0:T(1024)(128)(4,1)}, pred[1536]{0:T(1024)(128)(4,1)S(1)}, u32[]{:S(2)}) copy-start(pred[1536]{0:T(1024)(128)(4,1)S(1)} %eq.91) | copy-start | bytes 4612
  82.1 29.6 %copy-start.49 = (pred[1536]{0:T(1024)(128)(4,1)}, pred[1536]{0:T(1024)(128)(4,1)S(1)}, u32[]{:S(2)}) copy-start(pred[1536]{0:T(1024)(128)(4,1)S(1)} %eq.93) | copy-start | bytes 4612
  82.1 29.5 %copy-start.51 = (pred[1536]{0:T(1024)(128)(4,1)}, pred[1536]{0:T(1024)(128)(4,1)S(1)}, u32[]{:S(2)}) copy-start(pred[1536]{0:T(1024)(128)(4,1)S(1)} %eq.95) | copy-start | bytes 4612
  82.2 29.5 %copy-start.53 = (pred[1536]{0:T(1024)(128)(4,1)}, pred[1536]{0:T(1024)(128)(4,1)S(1)}, u32[]{:S(2)}) copy-start(pred[1536]{0:T(1024)(128)(4,1)S(1)} %eq.97) | copy-start | bytes 4612
  82.2 29.5 %copy-start.55 = (pred[1536]{0:T(1024)(128)(4,1)}, pred[1536]{0:T(1024)(128)(4,1)S(1)}, u32[]{:S(2)}) copy-start(pred[1536]{0:T(1024)(128)(4,1)S(1)} %eq.99) | copy-start | bytes 4612
  130.3 4.6 copy-start.33
  130.4 4.6 copy-start.87
  130.4 18.9 %copy-start.12 = (f32[256,100]{1,0:T(8,128)S(1)}, f32[256,100]{1,0:T(8,128)}, u32[]{:S(2)}) copy-start(f32[256,100]{1,0:T(8,128)} %gather_fusion.6) | copy-start | bytes 307204
  130.4 18.9 %copy-start.85 = (pred[4,64]{1,0:T(4,128)(4,1)S(1)}, pred[4,64]{1,0:T(4,128)(4,1)}, u32[]{:S(2)}) copy-start(pred[4,64]{1,0:T(4,128)(4,1)} %copy-done.84) | copy-start | bytes 772
  130.4 34.1 %copy-start.35 = (f32[375,125]{1,0:T(8,128)S(1)}, f32[375,125]{1,0:T(8,128)}, u32[]{:S(2)}) copy-start(f32[375,125]{1,0:T(8,128)} %constant.770.clone) | copy-start | bytes 562504
  150.0 23.6 %collective-permute-start.4 = (f32[100,64]{0,1:T(8,128)}, f32[100,64]{0,1:T(8,128)}, u32[]{:S(2)}, u32[]{:S(2)}) collective-permute-start(f32[100,64]{0,1:T(8,128)} %get-tuple-element.368), channel_id=1, source_target_pairs={{0,496},{8,504},{16,0},{24,8},{32,16},{40,24},{48,32},{56,40},{64,... | collective-permute-start | bytes 76808 | tf_op jit(solution)/shard_map/ppermute | solution.py:16
  156.6 17.8 %collective-permute-start.5 = (f32[100,64]{0,1:T(8,128)}, f32[100,64]{0,1:T(8,128)}, u32[]{:S(2)}, u32[]{:S(2)}) collective-permute-start(f32[100,64]{0,1:T(8,128)} %get-tuple-element.367), channel_id=1, source_target_pairs={{0,504},{8,0},{16,8},{24,16},{32,24},{40,32},{48,40},{56,48},{64,5... | collective-permute-start | bytes 76808 | tf_op jit(solution)/shard_map/ppermute | solution.py:16
  160.6 14.6 %collective-permute-start.6 = (f32[100,64]{0,1:T(8,128)}, f32[100,64]{0,1:T(8,128)}, u32[]{:S(2)}, u32[]{:S(2)}) collective-permute-start(f32[100,64]{0,1:T(8,128)} %get-tuple-element.366), channel_id=1, source_target_pairs={{0,8},{8,16},{16,24},{24,32},{32,40},{40,48},{48,56},{56,64},{64,7... | collective-permute-start | bytes 76808 | tf_op jit(solution)/shard_map/ppermute | solution.py:16
  162.5 13.4 %collective-permute-start.7 = (f32[100,64]{0,1:T(8,128)}, f32[100,64]{0,1:T(8,128)}, u32[]{:S(2)}, u32[]{:S(2)}) collective-permute-start(f32[100,64]{0,1:T(8,128)} %get-tuple-element.365), channel_id=1, source_target_pairs={{0,16},{8,24},{16,32},{24,40},{32,48},{40,56},{48,64},{56,72},{64,... | collective-permute-start | bytes 76808 | tf_op jit(solution)/shard_map/ppermute | solution.py:16
  192.8 4.2 copy-start.48
  192.8 4.2 copy-start.50
  192.8 4.2 copy-start.52
  192.8 4.2 copy-start.54
  192.8 4.2 copy-start.56
  201.1 3.0 copy-start.83
  201.1 3.0 copy-start.91
  201.1 4.0 copy-start.61
  201.1 4.0 copy-start.65
  201.1 4.0 copy-start.67
  223.2 463.4 %copy-start.1 = (s32[4096]{0:T(1024)S(1)}, s32[4096]{0:T(1024)}, u32[]{:S(2)}) copy-start(s32[4096]{0:T(1024)} %param.90) | copy-start | bytes 49156
  (61 other events, 91.8 us)
Sparse Core Ops, SparseCore 0:
  212.9 472.4 all-reduce.1
where the time goes:
time: 695 us; the launch traced here: 693 us
  waiting for transfers between devices  458 us (66%)
  local copies, waits for them, and re-layouts  107 us (15%)
  other arithmetic  41.6 us (6%)
  starting transfers between devices  36.7 us (5%)
  blocking collectives  30.3 us (4%)
  between operations  16 us (2%)
    psum x1, waiting for transfers between devices, body(): grad_total = grad_total + lax.psum(partial_value, ('dom', 'elem'))  458 us
    ppermute x8, starting transfers between devices, shifted(): lax.ppermute(shard, axis, [(i, (i + by) % length) for i in range(length)])  36.7 us
    rev x8, local copies, waits for them, and re-layouts, orient_faces(): variant = variant[:, :, ::-1]  33.3 us
    all_gather x2, blocking collectives, body(): lax.all_gather(jnp.take(flat_traces, intra_send, axis=1), 'elem', axis=1,...  30.3 us
    unnamed x242, local copies, waits for them, and re-layouts  22.2 us
  transfers between devices with their start and end apart: 9, of which 1 were waited for; matrix products, arithmetic and copies ran while one was open for 8% of the time, Pallas kernels for 0%

commit v1 on v0

v1 whole, which is shorter than its diff:
```python
import functools

import jax
import jax.numpy as jnp
import numpy as np
from jax import lax
from jax.experimental import pallas as pl
from jax.experimental.pallas import tpu as pltpu
from jax.sharding import PartitionSpec as P

DT_STEP = 0.1
SECTION_A = (-1.514183444257, -1.697784692471)
SECTION_B = (0.1530572479681, 0.6994504559488)
OFFSETS = (-2, -1, 1, 2)
ELEM_ORDER = (1, 7, 2, 6, 3, 5, 4)
N_ELEM, N_DOM, NX, NZ = 8, 64, 4, 16
OWN, FAR = 12, 20
CHUNKS = 24
ROWS = 104
F32 = jnp.float32
I32 = jnp.int32
FACE_NODE = ((0, 5, 1), (100, 5, 1), (0, 25, 1), (20, 25, 1), (0, 25, 5), (4, 25, 5))
MESH = pl.DeviceIdType.MESH


def lobatto_tables():
    node_points = np.array([-1.0, -np.sqrt(3.0 / 7.0), 0.0, np.sqrt(3.0 / 7.0), 1.0])
    quad_line = np.array([0.1, 49.0 / 90.0, 32.0 / 45.0, 49.0 / 90.0, 0.1])
    bary_weight = np.array(
        [
            1.0 / np.prod([node_points[j] - node_points[k] for k in range(5) if k != j])
            for j in range(5)
        ]
    )
    line_deriv = np.zeros((5, 5))
    for i in range(5):
        for j in range(5):
            if i != j:
                line_deriv[i, j] = (
                    bary_weight[j] / bary_weight[i] / (node_points[i] - node_points[j])
                )
        line_deriv[i, i] = -np.sum(line_deriv[i])
    return (line_deriv, quad_line)


def constant_tables():
    line_deriv, quad_line = lobatto_tables()
    eye = np.eye(5)
    stack = np.zeros((3, 128, 125), np.float32)
    stack[0, :125] = np.kron(np.kron(line_deriv, eye), eye)
    stack[1, :125] = np.kron(np.kron(eye, line_deriv), eye)
    stack[2, :125] = np.kron(np.kron(eye, eye), line_deriv)
    stack = stack.reshape(384, 125)
    high = stack.astype(jnp.bfloat16)
    low = (stack - high.astype(np.float32)).astype(jnp.bfloat16)
    weights = np.broadcast_to(np.outer(quad_line, quad_line).reshape(25, 1), (25, 128))
    grid = np.arange(25).reshape(5, 5)
    perm = np.zeros((8, 32, 64), np.float32)
    for symmetry in range(8):
        variant = grid
        if symmetry & 4:
            variant = variant.T
        if symmetry & 1:
            variant = variant[::-1]
        if symmetry & 2:
            variant = variant[:, ::-1]
        for row, source in enumerate(variant.reshape(-1)):
            perm[symmetry, row, source] = 1.0
            perm[symmetry, row, 32 + source] = 1.0
    return (
        jnp.asarray(high),
        jnp.asarray(low),
        jnp.asarray(perm.reshape(256, 64), jnp.bfloat16),
        jnp.asarray(weights, F32),
    )


def lane_take(values, index):
    return jnp.take_along_axis(values, index, axis=1, mode="promise_in_bounds")


def split(values):
    high = values.astype(jnp.bfloat16)
    return high, (values - high.astype(F32)).astype(jnp.bfloat16)


def rows_of(row, count):
    return jnp.broadcast_to(row, (count, 128))


def iota(shape, dim):
    return lax.broadcasted_iota(I32, shape, dim)


def kernel(
    adj_in, reg_in, metric, link, orient, isend, psend, wface, wpatch, pcount, amp, decay,
    aux_in, auxr_in, fwd, dhigh, dlow, perm, weights,
    adj_out, reg_out, aux_out, auxr_out, grad_out,
    A, R, S, pool, sendb, G, lift, wall, wslot, uslot, ampb, decb, T, Trecv, onehot, X, Xrecv, Z, Zrecv,
    load_sem, own_sem, si_sem, ri_sem, sp_sem, rp_sem, sg_sem, rg_sem, sx_sem, rx_sem, sz_sem, rz_sem,
):
    q = lax.axis_index("dom")
    e = lax.axis_index("elem")
    z, x = q // NX, q % NX

    def at_elem(by):
        return (q, (e + by) % N_ELEM)

    def at_dom(by):
        return ((q + by + N_DOM) % N_DOM, e)

    def at_x(by):
        return (z * NX + (x + by) % NX, e)

    def at_z(by):
        return (((z + by) % NZ) * NX + x, e)

    partners = (
        [at_elem(m) for m in range(1, N_ELEM)]
        + [at_dom(o) for o in OFFSETS]
        + [at_x(m) for m in range(1, NX)]
        + [at_z(m) for m in range(1, NZ)]
    )
    barrier = pltpu.get_barrier_semaphore()
    for partner in partners:
        pl.semaphore_signal(barrier, inc=1, device_id=partner, device_id_type=MESH)

    load_a = pltpu.make_async_copy(adj_in, A, load_sem.at[0])
    load_r = pltpu.make_async_copy(reg_in, R, load_sem.at[1])
    load_a.start()
    load_r.start()

    A2, S2 = A.reshape(1000, 128), S.reshape(1000, 128)
    for row in range(3):
        sendb[0, row, pl.ds(100, 4), :] = jnp.zeros((4, 128), F32)
        sendb[1, row, pl.ds(100, 4), :] = jnp.zeros((4, 128), F32)

    send_rows = [
        isend[...],
        jnp.concatenate([psend[0:1, :], psend[1:2, :]], axis=1),
        jnp.concatenate([psend[2:3, :], psend[3:4, :]], axis=1),
    ]

    def make_traces(s):
        lanes = [rows_of(row & 127, 8) for row in send_rows]
        faces = [rows_of(row >> 8, 8) for row in send_rows]
        halves = [rows_of((row >> 7) & 1, 4) == 1 for row in send_rows]

        def one_row(a, carry):
            for b in range(5):
                kept = [jnp.zeros((8, 128), F32)] * 3
                for f in range(6):
                    n0, na, nb = FACE_NODE[f]
                    v = A[n0 + na * a + nb * b]
                    for h in range(2):
                        pool[s, 2 * f + h, pl.ds(20 * a + 4 * b, 4), :] = v[4 * h : 4 * h + 4]
                    for t in range(3):
                        kept[t] = jnp.where(faces[t] == f, lane_take(v, lanes[t]), kept[t])
                for t in range(3):
                    sendb[s, t, pl.ds(20 * a + 4 * b, 4), :] = jnp.where(
                        halves[t], kept[t][4:8], kept[t][0:4]
                    )
            return carry

        lax.fori_loop(0, 5, one_row, 0)

    def start_sends(s):
        own = pltpu.make_async_copy(
            sendb.at[s, 0], pool.at[s, OWN + e, pl.ds(0, ROWS)], own_sem.at[s]
        )
        own.start()
        inner, outer = {}, []
        for m in ELEM_ORDER:
            inner[m] = pltpu.make_async_remote_copy(
                src_ref=sendb.at[s, 0],
                dst_ref=pool.at[s, OWN + e, pl.ds(0, ROWS)],
                send_sem=si_sem.at[s, m],
                recv_sem=ri_sem.at[s, m],
                device_id=at_elem(m),
                device_id_type=MESH,
            )
        for r, o in enumerate(OFFSETS):
            outer.append(
                pltpu.make_async_remote_copy(
                    src_ref=sendb.at[s, 1 + r // 2],
                    dst_ref=pool.at[s, FAR + r, pl.ds(0, ROWS)],
                    send_sem=sp_sem.at[s, r],
                    recv_sem=rp_sem.at[s, r],
                    device_id=at_dom(o),
                    device_id_type=MESH,
                )
            )
        for copy in [inner[4], outer[0], outer[3], inner[3], inner[5], outer[1], outer[2]]:
            copy.start()
        for m in (2, 6, 1, 7):
            inner[m].start()
        return own, inner, outer

    def component(s, chunk, c):
        return pool[s, chunk, pl.ds(c, 32, stride=4), :]

    link_all = link[...]
    near_link = jnp.where(link_all < 0, 0, link_all)
    far = near_link >= 2560
    lane_all = jnp.where(far, near_link - 2560, near_link) & 127
    chunk_all = jnp.where(far, FAR + ((near_link - 2560) >> 6), near_link >> 7)

    def face_row(table, f, h):
        return table[f : f + 1, 128 * h : 128 * h + 128]

    def gather_pass(s, chunks, first):
        for f in range(6):
            sign = -1.0 if f % 2 == 0 else 1.0
            kept, lane, chunk_of = [], [], []
            for h in range(2):
                kept.append(jnp.zeros((32, 128), F32) if first else G[2 * f + h])
                lane.append(rows_of(face_row(lane_all, f, h), 32))
                chunk_of.append(rows_of(face_row(chunk_all, f, h), 32))
            for chunk in chunks:
                values = component(s, chunk, 0) - sign * component(s, chunk, 1 + f // 2)
                for h in range(2):
                    kept[h] = jnp.where(chunk_of[h] == chunk, lane_take(values, lane[h]), kept[h])
            for h in range(2):
                G[2 * f + h] = kept[h]

    def volume(s):
        def comp(c):
            return jnp.concatenate(
                [A2[pl.ds(4 * h + c, 125, stride=8), :] for h in range(2)], axis=1
            )

        def precise(high_part, low_part, values):
            high, low = split(values)
            dot = functools.partial(jnp.dot, preferred_element_type=F32)
            return dot(high_part, high) + (dot(high_part, low) + dot(low_part, high))

        pressure = precise(dhigh[...], dlow[...], comp(0))
        total = None
        for d in range(3):
            scale = metric[d : d + 1, :]
            term = scale * precise(
                dhigh[pl.ds(128 * d, 128), :], dlow[pl.ds(128 * d, 128), :], comp(1 + d)
            )
            total = term if total is None else total + term
            grad = -scale * pressure[128 * d : 128 * d + 125]
            for h in range(2):
                S2[pl.ds(4 * h + 1 + d, 125, stride=8), :] = grad[:, 128 * h : 128 * h + 128]
        for h in range(2):
            S2[pl.ds(4 * h, 125, stride=8), :] = -total[0:125, 128 * h : 128 * h + 128]

    def add_rows(start, count, stride, values):
        where = pl.ds(start, count, stride=stride)
        S2[where, :] = S2[where, :] + values

    def fluxes(s):
        for f in range(6):
            d = f // 2
            sign = -1.0 if f % 2 == 0 else 1.0
            live_row = iota((32, 128), 0) < 25
            pair = jnp.concatenate(
                [jnp.where(live_row, G[2 * f + h], 0.0) for h in range(2)], axis=1
            )
            high, low = split(pair)
            variants = jnp.dot(
                perm[...], jnp.concatenate([high, low], axis=0), preferred_element_type=F32
            )
            for h in range(2):
                lanes = slice(128 * h, 128 * h + 128)
                turn = rows_of(face_row(orient, f, h), 32)
                near = variants[0:32, lanes]
                for symmetry in range(1, 8):
                    near = jnp.where(
                        turn == symmetry, variants[32 * symmetry : 32 * symmetry + 32, lanes], near
                    )
                p_own = component(s, 2 * f + h, 0)
                un_own = sign * component(s, 2 * f + h, 1 + d)
                wall_here = lane_take(wall[...], wslot[2 * f + h])
                is_wall = rows_of(face_row(link, f, h), 32) < 0
                near = jnp.where(is_wall, p_own + un_own - 2.0 * wall_here, near)
                lifted = (5.0 * metric[d : d + 1, lanes]) * (near - (p_own - un_own))
                n0, _, nb = FACE_NODE[f]
                for c, scale in ((0, 1.0), (1 + d, -sign)):
                    base = 8 * n0 + 4 * h + c
                    part = lifted if scale > 0 else -lifted
                    if d != 1:
                        add_rows(base, 25, 8 * nb, part[0:25])
                    else:
                        slot = 0 if scale > 0 else 1
                        lift[slot] = part
                        for a in range(5):
                            add_rows(base + 200 * a, 5, 8, lift[slot, pl.ds(5 * a, 5), :])

    def update(s):
        coef_a, coef_b = SECTION_A[s], SECTION_B[s]

        def step(i, carry):
            at = pl.ds(25 * i, 25)
            new = coef_a * R[at] + DT_STEP * S[at]
            R[at] = new
            A[at] = A[at] + coef_b * new
            return carry

        lax.fori_loop(0, 5, step, 0, unroll=True)

    patch = wpatch[...]
    live = wface[...] >= 0

    def patch_tables():
        lane8, chunk8 = rows_of(patch & 127, 8), rows_of(patch >> 7, 8)
        lane32 = rows_of(patch & 127, 32)
        counts = lane_take(pcount[...], lane32).astype(F32)
        mine = iota((32, 128), 0) == rows_of(patch >> 7, 32)
        count = jnp.sum(jnp.where(mine, counts, 0.0), axis=0, keepdims=True)
        active = (iota((8, 128), 0).astype(F32) < rows_of(count, 8)) & rows_of(live, 8)
        gain = jnp.zeros((8, 128), F32)
        rate = jnp.zeros((8, 128), F32)
        for c in range(32):
            lanes = pl.ds(128 * c, 128)
            ampb[pl.ds(0, 6), :] = amp[:, lanes]
            decb[pl.ds(0, 6), :] = decay[:, lanes]
            gain = jnp.where(chunk8 == c, lane_take(ampb[...], lane8), gain)
            rate = jnp.where(chunk8 == c, lane_take(decb[...], lane8), rate)
        six = iota((8, 128), 0) < 6
        active = active & six
        gain = jnp.where(active, gain, 0.0)
        rate = jnp.where(six, rate, 0.0)
        return jnp.where(active, 1.0, 0.0), gain, rate

    def slot_tables():
        face_column = jnp.transpose(rows_of(wface[...].astype(F32), 128))
        slot_column = iota((128, 128), 0).astype(F32)
        lane = iota((128, 128), 1).astype(F32)
        for j in range(12):
            hit = jnp.where(face_column == lane + 128.0 * j, slot_column, 0.0)
            wslot[j] = rows_of(jnp.sum(hit, axis=0, keepdims=True), 32).astype(I32)

    def walls(s, active, gain, rate):
        face_lane = rows_of(wface[...] & 127, 32)
        face_chunk = rows_of(wface[...] >> 7, 32)
        un = jnp.zeros((32, 128), F32)
        for f in range(6):
            sign = -1.0 if f % 2 == 0 else 1.0
            for h in range(2):
                taken = lane_take(component(s, 2 * f + h, 1 + f // 2), face_lane)
                un = jnp.where(face_chunk == 2 * f + h, sign * taken, un)
        uslot[...] = un
        un = uslot[pl.ds(0, 25), :]
        value = jnp.zeros((25, 128), F32)
        weighted = weights[...] * un
        aux_from, auxr_from = (aux_in, auxr_in) if s == 0 else (aux_out, auxr_out)
        for k in range(6):
            aux = aux_from[k]
            value = value + gain[k : k + 1] * aux
            fresh = jnp.sum(weighted * fwd[k, :, s, :].astype(F32), axis=0, keepdims=True)
            fresh = (SECTION_B[s] * DT_STEP) * active[k : k + 1] * fresh
            T[pl.ds(k, 1), :] = fresh if s == 0 else T[pl.ds(k, 1), :] + fresh
            rate_k = active[k : k + 1] * (un - rate[k : k + 1] * aux)
            new = SECTION_A[s] * auxr_from[k] + DT_STEP * rate_k
            auxr_out[k] = new
            aux_out[k] = aux + SECTION_B[s] * new
        wall[pl.ds(0, 25), :] = value

    def wait_halo(s, copies):
        own, inner, outer = copies
        own.wait()
        for m in ELEM_ORDER:
            inner[m].wait_recv()
        for copy in outer:
            copy.wait_recv()

    def wait_sent(copies):
        _, inner, outer = copies
        for m in ELEM_ORDER:
            inner[m].wait_send()
        for copy in outer:
            copy.wait_send()

    load_a.wait()
    make_traces(0)
    pl.semaphore_wait(barrier, len(partners))
    copies = start_sends(0)
    active, gain, rate = patch_tables()
    slot_tables()
    T[...] = jnp.zeros((8, 128), F32)
    T[pl.ds(6, 1), :] = patch.astype(F32)
    walls(0, active, gain, rate)
    volume(0)
    gather_pass(0, range(OWN), True)
    load_r.wait()
    wait_halo(0, copies)
    gather_pass(0, range(OWN, CHUNKS), False)
    fluxes(0)
    update(0)

    make_traces(1)
    copies_1 = start_sends(1)
    walls(1, active, gain, rate)
    Trecv[e] = T[...]
    sums = []
    for m in ELEM_ORDER:
        copy = pltpu.make_async_remote_copy(
            src_ref=T,
            dst_ref=Trecv.at[e],
            send_sem=sg_sem.at[m],
            recv_sem=rg_sem.at[m],
            device_id=at_elem(m),
            device_id_type=MESH,
        )
        copy.start()
        sums.append(copy)
    volume(1)
    gather_pass(1, range(OWN), True)

    for copy in sums:
        copy.wait_recv()
    column = iota((512, 128), 0).astype(F32)
    highs, lows = [], []
    for j in range(N_ELEM):
        ids = Trecv[j, pl.ds(6, 1), :].astype(I32)
        at = ((ids >> 6) & 3) * 128 + (ids >> 8) * 8 + (ids & 7)
        at = jnp.where(((ids >> 3) & 7) == e, at, -1).astype(F32)
        onehot[:, pl.ds(128 * j, 128)] = jnp.where(column == rows_of(at, 512), 1.0, 0.0).astype(
            jnp.bfloat16
        )
        high, low = split(Trecv[j])
        highs.append(high)
        lows.append(low)
    terms = jnp.concatenate(
        [jnp.concatenate(highs, axis=1), jnp.concatenate(lows, axis=1)], axis=0
    )
    binned = lax.dot_general(
        terms, onehot[...], (((1,), (1,)), ((), ())), preferred_element_type=F32
    )
    binned = binned[0:8] + binned[8:16]
    for j in range(NX):
        X[j] = binned[:, 128 * j : 128 * j + 128]
    Xrecv[x] = X[x]
    sums_x = []
    for m in range(1, NX):
        copy = pltpu.make_async_remote_copy(
            src_ref=X.at[(x + m) % NX],
            dst_ref=Xrecv.at[x],
            send_sem=sx_sem.at[m],
            recv_sem=rx_sem.at[m],
            device_id=at_x(m),
            device_id_type=MESH,
        )
        copy.start()
        sums_x.append(copy)

    wait_halo(1, copies_1)
    gather_pass(1, range(OWN, CHUNKS), False)

    for copy in sums_x:
        copy.wait_recv()
    summed = Xrecv[0] + Xrecv[1] + Xrecv[2] + Xrecv[3]
    lane16 = iota((8, 128), 1)
    for g in range(2):
        index = (8 * g + iota((8, 128), 0)) * 8 + (lane16 & 7)
        block = jnp.zeros((8, 128), F32)
        for k in range(6):
            block = jnp.where(
                (lane16 >> 3) == k, lane_take(rows_of(summed[k : k + 1], 8), index), block
            )
        for i in range(8):
            Z[8 * g + i] = block[i : i + 1]
    Zrecv[z] = Z[z]
    sums_z = []
    for m in range(1, NZ):
        copy = pltpu.make_async_remote_copy(
            src_ref=Z.at[(z + m) % NZ],
            dst_ref=Zrecv.at[z],
            send_sem=sz_sem.at[m],
            recv_sem=rz_sem.at[m],
            device_id=at_z(m),
            device_id_type=MESH,
        )
        copy.start()
        sums_z.append(copy)

    fluxes(1)
    update(1)
    store_a = pltpu.make_async_copy(A, adj_out, load_sem.at[0])
    store_r = pltpu.make_async_copy(R, reg_out, load_sem.at[1])
    store_a.start()
    store_r.start()

    for copy in sums_z:
        copy.wait_recv()
    row = Zrecv[0]
    for j in range(1, NZ):
        row = row + Zrecv[j]
    index = (iota((8, 128), 0) + 8 * iota((8, 128), 1)) & 127
    grad_out[...] = lane_take(rows_of(row, 8), index)[:, 0:6]

    wait_sent(copies)
    wait_sent(copies_1)
    for copy in sums + sums_x + sums_z:
        copy.wait_send()
    store_a.wait()
    store_r.wait()


def body(
    adjoint,
    adjoint_reg,
    metric,
    face_link,
    orient,
    intra_send,
    part_send,
    wall_face,
    wall_patch,
    pole_count,
    amplitude,
    pole_decay,
    wall_aux,
    wall_aux_reg,
    forward_aux,
):
    def packed(fields):
        return fields.reshape(4, 125, 2, 128).transpose(1, 2, 0, 3).reshape(125, 8, 128)

    def unpacked(nodes):
        return nodes.reshape(125, 2, 4, 128).transpose(2, 0, 1, 3).reshape(4, 125, 256)

    vmem = pl.BlockSpec(memory_space=pltpu.VMEM)
    hbm = pl.BlockSpec(memory_space=pl.ANY)
    dma = pltpu.SemaphoreType.DMA
    adj, reg, aux, auxr, grad = pl.pallas_call(
        kernel,
        out_shape=[
            jax.ShapeDtypeStruct((125, 8, 128), F32),
            jax.ShapeDtypeStruct((125, 8, 128), F32),
            jax.ShapeDtypeStruct((6, 25, 128), F32),
            jax.ShapeDtypeStruct((6, 25, 128), F32),
            jax.ShapeDtypeStruct((8, 6), F32),
        ],
        in_specs=[hbm, hbm] + [vmem] * 17,
        out_specs=[hbm, hbm] + [vmem] * 3,
        scratch_shapes=[
            pltpu.VMEM((125, 8, 128), F32),
            pltpu.VMEM((125, 8, 128), F32),
            pltpu.VMEM((125, 8, 128), F32),
            pltpu.VMEM((2, CHUNKS, 128, 128), F32),
            pltpu.VMEM((2, 3, ROWS, 128), F32),
            pltpu.VMEM((12, 32, 128), F32),
            pltpu.VMEM((2, 32, 128), F32),
            pltpu.VMEM((32, 128), F32),
            pltpu.VMEM((12, 32, 128), I32),
            pltpu.VMEM((32, 128), F32),
            pltpu.VMEM((8, 128), F32),
            pltpu.VMEM((8, 128), F32),
            pltpu.VMEM((8, 128), F32),
            pltpu.VMEM((N_ELEM, 8, 128), F32),
            pltpu.VMEM((512, 1024), jnp.bfloat16),
            pltpu.VMEM((NX, 8, 128), F32),
            pltpu.VMEM((NX, 8, 128), F32),
            pltpu.VMEM((NZ, 1, 128), F32),
            pltpu.VMEM((NZ, 1, 128), F32),
            dma((2,)),
            dma((2,)),
            dma((2, N_ELEM)),
            dma((2, N_ELEM)),
            dma((2, 4)),
            dma((2, 4)),
            dma((N_ELEM,)),
            dma((N_ELEM,)),
            dma((NX,)),
            dma((NX,)),
            dma((NZ,)),
            dma((NZ,)),
        ],
        compiler_params=pltpu.CompilerParams(
            collective_id=0, has_side_effects=True, vmem_limit_bytes=48 * 1024 * 1024
        ),
        cost_estimate=pl.CostEstimate(flops=400_000_000, bytes_accessed=3_000_000, transcendentals=0),
    )(
        packed(adjoint),
        packed(adjoint_reg),
        metric,
        face_link,
        orient,
        intra_send.reshape(1, 128),
        part_send,
        wall_face.reshape(1, 128),
        wall_patch.reshape(1, 128),
        pole_count.reshape(32, 128),
        amplitude.T,
        pole_decay.T,
        wall_aux,
        wall_aux_reg,
        forward_aux.transpose(1, 2, 0, 3),
        *constant_tables(),
    )
    return (unpacked(adj), unpacked(reg), aux, auxr, grad)


def solution(mesh):
    both = ("dom", "elem")
    in_specs = (
        P(None, None, both),
        P(None, None, both),
        P(None, both),
        P(None, both),
        P(None, both),
        P(both),
        P(None, both),
        P(both),
        P(both),
        P(),
        P(),
        P(),
        P(None, None, both),
        P(None, None, both),
        P(None, None, None, both),
    )
    out_specs = (
        P(None, None, both),
        P(None, None, both),
        P(None, None, both),
        P(None, None, both),
        P(both, None),
    )
    return jax.shard_map(body, mesh=mesh, in_specs=in_specs, out_specs=out_specs, check_vma=False)
```

time: 695 us -> 62.6 us (0.09)
  waiting for transfers between devices: 458 us -> 0 us
  local copies, waits for them, and re-layouts: 107 us -> 17.4 us
  Pallas kernels: 0 us -> 43.7 us
  other arithmetic: 41.6 us -> 0 us
  starting transfers between devices: 36.7 us -> 0 us
  blocking collectives: 30.3 us -> 0 us
  between operations: 16 us -> 0.69 us
    psum x1 -> x0, waiting for transfers between devices: 458 us -> none  [body(): grad_total = grad_total + lax.psum(partial_value, ('dom', 'elem'))]
    pallas_call x0 -> x1, Pallas kernels: none -> 43.7 us  [body(): pl.pallas_call(kernel, out_shape=[jax.ShapeDtypeStruct((125, 8, 128), F32...]
    ppermute x8 -> x0, starting transfers between devices: 36.7 us -> none  [shifted(): lax.ppermute(shard, axis, [(i, (i + by) % length) for i in range(length)])]
    rev x8 -> x0, local copies, waits for them, and re-layouts: 33.3 us -> none  [orient_faces(): variant = variant[:, :, ::-1]]
    all_gather x2 -> x0, blocking collectives: 30.3 us -> none  [body(): lax.all_gather(jnp.take(flat_traces, intra_send, axis=1), 'elem', axis=1,...]
    gather x13 -> x0, local copies, waits for them, and re-layouts: 15.3 us -> none  [the longest x2 5.17 us: section_update(): jnp.take(trace_pool, jnp.where(is_wall, 0, link_flat), axis=1)]
    scatter-add x18 -> x0, other arithmetic: 12.3 us -> none  [the longest x8 7.95 us: lift_faces(): grid_residual = grid_residual.at[(0,) + position].add(lifted)]
    slice x10 -> x0, local copies, waits for them, and re-layouts: 9.26 us -> none  [the longest x2 5.34 us: section_update(): own_trace[0]]
  transfers between devices with their start and end apart: 9 -> 0, of which waited for: 1 -> 0; matrix products, arithmetic and copies ran while one was open for 8% -> 0% of each run, Pallas kernels for 0% -> 0%
where the time goes in v1:
time: 62.6 us; the launch traced here: 61.8 us
  Pallas kernels  43.7 us (70%)
  local copies, waits for them, and re-layouts  17.4 us (28%)
  between operations  0.69 us (1%)
    pallas_call x1, Pallas kernels, body(): pl.pallas_call(kernel, out_shape=[jax.ShapeDtypeStruct((125, 8, 128), F32...  43.7 us
    unnamed x43, local copies, waits for them, and re-layouts  17.4 us

profile of v1, /device:TPU:1, one launch (start us, length us, event | category | flops | bytes accessed | tf_op | source)
XLA Modules:
  0.0 61.8 jit_solution(10873572032589634305)
XLA Ops:
  0.6 0.0 copy-start.10
  0.6 0.0 copy-start.16
  0.7 0.0 copy-start.17
  0.7 0.7 %copy-done.10 = s32[4096]{0:T(1024)S(1)} copy-done((s32[4096]{0:T(1024)S(1)}, s32[4096]{0:T(1024)}, u32[]{:S(2)}) %copy-start.10) | copy-done | bytes 16408
  1.4 0.0 copy-done.16
  1.4 0.0 copy-done.17
  1.4 0.0 copy-start
  1.4 1.0 %copy-done = f32[4,125,256]{2,0,1:T(4,128)S(1)} copy-done((f32[4,125,256]{2,0,1:T(4,128)S(1)}, f32[4,125,256]{2,0,1:T(4,128)}, u32[]{:S(2)}) %copy-start) | copy-done | bytes 512024
  2.4 0.0 copy-start.1
  2.4 1.0 %copy-done.1 = f32[4,125,256]{2,0,1:T(4,128)S(1)} copy-done((f32[4,125,256]{2,0,1:T(4,128)S(1)}, f32[4,125,256]{2,0,1:T(4,128)}, u32[]{:S(2)}) %copy-start.1) | copy-done | bytes 512024
  3.4 0.0 copy-start.2
  3.4 0.9 %copy-done.2 = f32[4096,6]{0,1:T(8,128)S(1)} copy-done((f32[4096,6]{0,1:T(8,128)S(1)}, f32[4096,6]{0,1:T(8,128)}, u32[]{:S(2)}) %copy-start.2) | copy-done | bytes 98328
  4.3 0.0 copy-start.3
  4.3 0.9 %copy-done.3 = f32[4096,6]{0,1:T(8,128)S(1)} copy-done((f32[4096,6]{0,1:T(8,128)S(1)}, f32[4096,6]{0,1:T(8,128)}, u32[]{:S(2)}) %copy-start.3) | copy-done | bytes 98328
  5.2 0.0 copy-start.4
  5.2 0.9 %copy-done.4 = f32[6,25,128]{2,1,0:T(8,128)S(1)} copy-done((f32[6,25,128]{2,1,0:T(8,128)S(1)}, f32[6,25,128]{2,1,0:T(8,128)}, u32[]{:S(2)}) %copy-start.4) | copy-done | bytes 76824
  6.1 0.0 copy-start.5
  6.1 0.9 %copy-done.5 = f32[6,25,128]{2,1,0:T(8,128)S(1)} copy-done((f32[6,25,128]{2,1,0:T(8,128)S(1)}, f32[6,25,128]{2,1,0:T(8,128)}, u32[]{:S(2)}) %copy-start.5) | copy-done | bytes 76824
  7.0 0.0 copy-start.6
  7.0 0.9 %copy-done.6 = bf16[384,125]{1,0:T(8,128)(2,1)S(1)} copy-done((bf16[384,125]{1,0:T(8,128)(2,1)S(1)}, bf16[384,125]{1,0:T(8,128)(2,1)}, u32[]{:S(2)}) %copy-start.6) | copy-done | bytes 96024
  7.9 0.0 copy-start.7
  7.9 0.9 %copy-done.7 = bf16[384,125]{1,0:T(8,128)(2,1)S(1)} copy-done((bf16[384,125]{1,0:T(8,128)(2,1)S(1)}, bf16[384,125]{1,0:T(8,128)(2,1)}, u32[]{:S(2)}) %copy-start.7) | copy-done | bytes 96024
  8.8 0.0 copy-start.8
  8.8 0.9 %copy-done.8 = bf16[2,6,25,128]{3,0,2,1:T(2,128)(2,1)S(1)} copy-done((bf16[2,6,25,128]{3,0,2,1:T(2,128)(2,1)S(1)}, bf16[2,6,25,128]{3,0,2,1:T(2,128)(2,1)}, u32[]{:S(2)}) %copy-start.8) | copy-done | bytes 76824
  9.7 0.0 copy-start.9
  9.7 0.8 %copy-done.9 = bf16[256,64]{1,0:T(8,128)(2,1)S(1)} copy-done((bf16[256,64]{1,0:T(8,128)(2,1)S(1)}, bf16[256,64]{1,0:T(8,128)(2,1)}, u32[]{:S(2)}) %copy-start.9) | copy-done | bytes 32792
  10.5 0.0 copy-start.11
  10.5 0.7 %copy-done.11 = f32[25,128]{1,0:T(8,128)S(1)} copy-done((f32[25,128]{1,0:T(8,128)S(1)}, f32[25,128]{1,0:T(8,128)}, u32[]{:S(2)}) %copy-start.11) | copy-done | bytes 12824
  11.3 0.0 copy-start.12
  11.3 0.7 %copy-done.12 = s32[6,256]{1,0:T(8,128)S(1)} copy-done((s32[6,256]{1,0:T(8,128)S(1)}, s32[6,256]{1,0:T(8,128)}, u32[]{:S(2)}) %copy-start.12) | copy-done | bytes 6168
  12.0 0.0 copy-start.13
  12.0 0.7 %copy-done.13 = s32[6,256]{1,0:T(8,128)S(1)} copy-done((s32[6,256]{1,0:T(8,128)S(1)}, s32[6,256]{1,0:T(8,128)}, u32[]{:S(2)}) %copy-start.13) | copy-done | bytes 6168
  12.7 0.0 copy-start.14
  12.7 0.7 %copy-done.14 = f32[3,256]{1,0:T(4,128)S(1)} copy-done((f32[3,256]{1,0:T(4,128)S(1)}, f32[3,256]{1,0:T(4,128)}, u32[]{:S(2)}) %copy-start.14) | copy-done | bytes 3096
  13.3 0.0 copy-start.15
  13.3 0.7 %copy-done.15 = s32[4,64]{1,0:T(4,128)S(1)} copy-done((s32[4,64]{1,0:T(4,128)S(1)}, s32[4,64]{1,0:T(4,128)}, u32[]{:S(2)}) %copy-start.15) | copy-done | bytes 1048
  14.0 0.0 copy-start.18
  14.0 0.7 %copy-done.18 = s32[128]{0:T(128)S(1)} copy-done((s32[128]{0:T(128)S(1)}, s32[128]{0:T(128)}, u32[]{:S(2)}) %copy-start.18) | copy-done | bytes 536
  14.7 43.7 %shard_map.218 = (f32[125,8,128]{2,1,0:T(8,128)S(1)}, f32[125,8,128]{2,1,0:T(8,128)S(1)}, f32[6,25,128]{2,1,0:T(8,128)S(1)}, f32[6,25,128]{2,1,0:T(8,128)S(1)}, f32[8,6]{1,0:T(8,128)S(1)}) custom-call(f32[125,8,128]{2,1,0:T(8,128)S(1)} %bitcast.27, f32[125,8,128]{2,1,0:T(8,128)S(1)} %bitcast.28, f32[3,256]{1,0:T(4,128)S(1)} %copy-done.14, ...), custom_call_target="tpu_custom_call" | custom-call | flops 400000000 | bytes 3000000 | tf_op jit(solution)/shard_map/pallas_call | solution.py:530
  58.4 0.8 %copy.33 = f32[4,125,256]{2,0,1:T(4,128)} copy(f32[4,125,256]{2,0,1:T(4,128)S(1)} %bitcast.30) | data formatting | bytes 1024000
  59.2 0.8 %copy.34 = f32[4,125,256]{2,0,1:T(4,128)} copy(f32[4,125,256]{2,0,1:T(4,128)S(1)} %bitcast.29) | data formatting | bytes 1024000
  60.0 0.6 %copy.35 = f32[6,25,128]{2,1,0:T(8,128)} copy(f32[6,25,128]{2,1,0:T(8,128)S(1)} %get-tuple-element.22) | data formatting | bytes 153600
  60.6 0.6 %copy.36 = f32[6,25,128]{2,1,0:T(8,128)} copy(f32[6,25,128]{2,1,0:T(8,128)S(1)} %get-tuple-element.23) | data formatting | bytes 153600
  61.3 0.6 copy.37
Async XLA Ops:
  0.6 0.7 %copy-start.10 = (s32[4096]{0:T(1024)S(1)}, s32[4096]{0:T(1024)}, u32[]{:S(2)}) copy-start(s32[4096]{0:T(1024)} %param.28) | copy-start | bytes 49156
  0.6 0.7 %copy-start.16 = (s32[128]{0:T(128)S(1)}, s32[128]{0:T(128)}, u32[]{:S(2)}) copy-start(s32[128]{0:T(128)} %param.24) | copy-start | bytes 1540
  0.7 0.7 %copy-start.17 = (s32[128]{0:T(128)S(1)}, s32[128]{0:T(128)}, u32[]{:S(2)}) copy-start(s32[128]{0:T(128)} %param.26) | copy-start | bytes 1540
  1.4 1.0 %copy-start = (f32[4,125,256]{2,0,1:T(4,128)S(1)}, f32[4,125,256]{2,0,1:T(4,128)}, u32[]{:S(2)}) copy-start(f32[4,125,256]{2,0,1:T(4,128)} %param.19) | copy-start | bytes 1536004
  2.4 1.0 %copy-start.1 = (f32[4,125,256]{2,0,1:T(4,128)S(1)}, f32[4,125,256]{2,0,1:T(4,128)}, u32[]{:S(2)}) copy-start(f32[4,125,256]{2,0,1:T(4,128)} %param.20) | copy-start | bytes 1536004
  3.4 0.9 %copy-start.2 = (f32[4096,6]{0,1:T(8,128)S(1)}, f32[4096,6]{0,1:T(8,128)}, u32[]{:S(2)}) copy-start(f32[4096,6]{0,1:T(8,128)} %param.29) | copy-start | bytes 294916
  4.3 0.9 %copy-start.3 = (f32[4096,6]{0,1:T(8,128)S(1)}, f32[4096,6]{0,1:T(8,128)}, u32[]{:S(2)}) copy-start(f32[4096,6]{0,1:T(8,128)} %param.30) | copy-start | bytes 294916
  5.2 0.9 %copy-start.4 = (f32[6,25,128]{2,1,0:T(8,128)S(1)}, f32[6,25,128]{2,1,0:T(8,128)}, u32[]{:S(2)}) copy-start(f32[6,25,128]{2,1,0:T(8,128)} %aux_in.1) | copy-start | bytes 230404
  6.1 0.9 %copy-start.5 = (f32[6,25,128]{2,1,0:T(8,128)S(1)}, f32[6,25,128]{2,1,0:T(8,128)}, u32[]{:S(2)}) copy-start(f32[6,25,128]{2,1,0:T(8,128)} %auxr_in.1) | copy-start | bytes 230404
  7.0 0.9 %copy-start.6 = (bf16[384,125]{1,0:T(8,128)(2,1)S(1)}, bf16[384,125]{1,0:T(8,128)(2,1)}, u32[]{:S(2)}) copy-start(bf16[384,125]{1,0:T(8,128)(2,1)} %constant.9.clone.dlow) | copy-start | bytes 288004
  7.9 0.9 %copy-start.7 = (bf16[384,125]{1,0:T(8,128)(2,1)S(1)}, bf16[384,125]{1,0:T(8,128)(2,1)}, u32[]{:S(2)}) copy-start(bf16[384,125]{1,0:T(8,128)(2,1)} %constant.8.clone.dhigh) | copy-start | bytes 288004
  8.8 0.9 %copy-start.8 = (bf16[2,6,25,128]{3,0,2,1:T(2,128)(2,1)S(1)}, bf16[2,6,25,128]{3,0,2,1:T(2,128)(2,1)}, u32[]{:S(2)}) copy-start(bf16[2,6,25,128]{3,0,2,1:T(2,128)(2,1)} %param.33) | copy-start | bytes 230404
  9.7 0.8 %copy-start.9 = (bf16[256,64]{1,0:T(8,128)(2,1)S(1)}, bf16[256,64]{1,0:T(8,128)(2,1)}, u32[]{:S(2)}) copy-start(bf16[256,64]{1,0:T(8,128)(2,1)} %constant.10.clone.perm) | copy-start | bytes 98308
  10.5 0.7 %copy-start.11 = (f32[25,128]{1,0:T(8,128)S(1)}, f32[25,128]{1,0:T(8,128)}, u32[]{:S(2)}) copy-start(f32[25,128]{1,0:T(8,128)} %constant.11.clone.weights) | copy-start | bytes 38404
  11.3 0.7 %copy-start.12 = (s32[6,256]{1,0:T(8,128)S(1)}, s32[6,256]{1,0:T(8,128)}, u32[]{:S(2)}) copy-start(s32[6,256]{1,0:T(8,128)} %link.1) | copy-start | bytes 18436
  12.0 0.7 %copy-start.13 = (s32[6,256]{1,0:T(8,128)S(1)}, s32[6,256]{1,0:T(8,128)}, u32[]{:S(2)}) copy-start(s32[6,256]{1,0:T(8,128)} %orient.1) | copy-start | bytes 18436
  12.7 0.7 %copy-start.14 = (f32[3,256]{1,0:T(4,128)S(1)}, f32[3,256]{1,0:T(4,128)}, u32[]{:S(2)}) copy-start(f32[3,256]{1,0:T(4,128)} %metric.1) | copy-start | bytes 9220
  13.3 0.7 %copy-start.15 = (s32[4,64]{1,0:T(4,128)S(1)}, s32[4,64]{1,0:T(4,128)}, u32[]{:S(2)}) copy-start(s32[4,64]{1,0:T(4,128)} %psend.1) | copy-start | bytes 3076
  14.0 0.7 %copy-start.18 = (s32[128]{0:T(128)S(1)}, s32[128]{0:T(128)}, u32[]{:S(2)}) copy-start(s32[128]{0:T(128)} %param.27) | copy-start | bytes 1540

commit v2 on v1

--- a/solution.py
+++ b/solution.py
@@ -12,10 +12,16 @@
 SECTION_A = (-1.514183444257, -1.697784692471)
 SECTION_B = (0.1530572479681, 0.6994504559488)
 OFFSETS = (-2, -1, 1, 2)
-ELEM_ORDER = (1, 7, 2, 6, 3, 5, 4)
+SAME_CORE = (4, 2, 6)
 N_ELEM, N_DOM, NX, NZ = 8, 64, 4, 16
 OWN, FAR = 12, 20
 CHUNKS = 24
+PLANE = tuple(
+    sorted(
+        ((dx, m) for dx in range(NX) for m in range(N_ELEM) if dx or m),
+        key=lambda at: -min(at[0], NX - at[0]) - min(at[1], N_ELEM - at[1]) / 2,
+    )
+)
 ROWS = 104
 F32 = jnp.float32
 I32 = jnp.int32
@@ -93,11 +99,12 @@
 
 
 def kernel(
-    adj_in, reg_in, metric, link, orient, isend, psend, wface, wpatch, pcount, amp, decay,
-    aux_in, auxr_in, fwd, dhigh, dlow, perm, weights,
-    adj_out, reg_out, aux_out, auxr_out, grad_out,
-    A, R, S, pool, sendb, G, lift, wall, wslot, uslot, ampb, decb, T, Trecv, onehot, X, Xrecv, Z, Zrecv,
-    load_sem, own_sem, si_sem, ri_sem, sp_sem, rp_sem, sg_sem, rg_sem, sx_sem, rx_sem, sz_sem, rz_sem,
+    adj_hbm, reg_hbm, metric_hbm, link_hbm, orient_hbm, isend_hbm, psend_hbm, wface_hbm, wpatch_hbm,
+    pcount_hbm, amp_hbm, decay_hbm, aux_hbm, auxr_hbm, fwd_hbm, dhigh_hbm, dlow_hbm, perm_hbm, weights_hbm,
+    A, R, aux_out, auxr_out, grad_out,
+    metric, link, orient, isend, psend, wface, wpatch, pcount, amp, decay, aux_in, auxr_in, fwd,
+    dhigh, dlow, perm, weights, S, pool, sendb, outb, G, lift, wall, wslot, uslot, ampb, decb, T, Trecv, onehot, Z, Zrecv,
+    load_sem, own_sem, si_sem, ri_sem, sr_sem, rr_sem, sp_sem, rp_sem, sg_sem, rg_sem, sz_sem, rz_sem,
 ):
     q = lax.axis_index("dom")
     e = lax.axis_index("elem")
@@ -109,39 +116,82 @@
     def at_dom(by):
         return ((q + by + N_DOM) % N_DOM, e)
 
-    def at_x(by):
-        return (z * NX + (x + by) % NX, e)
+    def at_xe(dx, m):
+        return (z * NX + (x + dx) % NX, (e + m) % N_ELEM)
 
     def at_z(by):
         return (((z + by) % NZ) * NX + x, e)
 
+    loads = {}
+    for number, (name, source, target) in enumerate(
+        (
+            ("isend", isend_hbm, isend),
+            ("psend", psend_hbm, psend),
+            ("A", adj_hbm, A),
+            ("wpatch", wpatch_hbm, wpatch),
+            ("wface", wface_hbm, wface),
+            ("link", link_hbm, link),
+            ("metric", metric_hbm, metric),
+            ("pcount", pcount_hbm, pcount),
+            ("amp", amp_hbm, amp),
+            ("decay", decay_hbm, decay),
+            ("weights", weights_hbm, weights),
+            ("aux", aux_hbm, aux_in),
+            ("auxr", auxr_hbm, auxr_in),
+            ("fwd", fwd_hbm, fwd),
+            ("dhigh", dhigh_hbm, dhigh),
+            ("dlow", dlow_hbm, dlow),
+            ("orient", orient_hbm, orient),
+            ("perm", perm_hbm, perm),
+            ("R", reg_hbm, R),
+        )
+    ):
+        loads[name] = pltpu.make_async_copy(source, target, load_sem.at[number])
+    first = ("isend", "psend", "A")
+    for name in first:
+        loads[name].start()
+
     partners = (
-        [at_elem(m) for m in range(1, N_ELEM)]
+        [at_xe(dx, m) for dx, m in PLANE]
         + [at_dom(o) for o in OFFSETS]
-        + [at_x(m) for m in range(1, NX)]
         + [at_z(m) for m in range(1, NZ)]
     )
     barrier = pltpu.get_barrier_semaphore()
     for partner in partners:
         pl.semaphore_signal(barrier, inc=1, device_id=partner, device_id_type=MESH)
-
-    load_a = pltpu.make_async_copy(adj_in, A, load_sem.at[0])
-    load_r = pltpu.make_async_copy(reg_in, R, load_sem.at[1])
-    load_a.start()
-    load_r.start()
+    for name in loads:
+        if name not in first:
+            loads[name].start()
+
+    def loaded(*names):
+        for name in names:
+            loads[name].wait()
 
     A2, S2 = A.reshape(1000, 128), S.reshape(1000, 128)
     for row in range(3):
         sendb[0, row, pl.ds(100, 4), :] = jnp.zeros((4, 128), F32)
         sendb[1, row, pl.ds(100, 4), :] = jnp.zeros((4, 128), F32)
 
+    loaded("isend", "psend", "A")
     send_rows = [
         isend[...],
         jnp.concatenate([psend[0:1, :], psend[1:2, :]], axis=1),
         jnp.concatenate([psend[2:3, :], psend[3:4, :]], axis=1),
     ]
 
-    def make_traces(s):
+    def own_traces(s):
+        def one_row(a, carry):
+            for b in range(5):
+                for f in range(6):
+                    n0, na, nb = FACE_NODE[f]
+                    v = A[n0 + na * a + nb * b]
+                    for h in range(2):
+                        pool[s, 2 * f + h, pl.ds(20 * a + 4 * b, 4), :] = v[4 * h : 4 * h + 4]
+            return carry
+
+        lax.fori_loop(0, 5, one_row, 0)
+
+    def sent_traces(s):
         lanes = [rows_of(row & 127, 8) for row in send_rows]
         faces = [rows_of(row >> 8, 8) for row in send_rows]
         halves = [rows_of((row >> 7) & 1, 4) == 1 for row in send_rows]
@@ -152,8 +202,6 @@
                 for f in range(6):
                     n0, na, nb = FACE_NODE[f]
                     v = A[n0 + na * a + nb * b]
-                    for h in range(2):
-                        pool[s, 2 * f + h, pl.ds(20 * a + 4 * b, 4), :] = v[4 * h : 4 * h + 4]
                     for t in range(3):
                         kept[t] = jnp.where(faces[t] == f, lane_take(v, lanes[t]), kept[t])
                 for t in range(3):
@@ -164,46 +212,104 @@
 
         lax.fori_loop(0, 5, one_row, 0)
 
-    def start_sends(s):
-        own = pltpu.make_async_copy(
-            sendb.at[s, 0], pool.at[s, OWN + e, pl.ds(0, ROWS)], own_sem.at[s]
-        )
-        own.start()
-        inner, outer = {}, []
-        for m in ELEM_ORDER:
-            inner[m] = pltpu.make_async_remote_copy(
+    def pack_outer(s):
+        left_short = iota((40, 128), 1) < 64
+        for t in range(2):
+            low, high = sendb[s, 1 + t, pl.ds(0, 64), :], sendb[s, 1 + t, pl.ds(64, 40), :]
+            outb[s, 2 * t] = low
+            outb[s, 2 * t, pl.ds(0, 40), :] = jnp.where(
+                left_short, low[0:40], pltpu.roll(high, 64, 1)
+            )
+            turned = pltpu.roll(low, 64, 1)
+            outb[s, 2 * t + 1] = turned
+            outb[s, 2 * t + 1, pl.ds(0, 40), :] = jnp.where(left_short, turned[0:40], high)
+
+    sibling = (q, e + 1 - 2 * (e % 2))
+
+    def block_of(m):
+        return OWN + (e + N_ELEM - m) % N_ELEM
+
+    def inner_copies(s):
+        return {
+            m: pltpu.make_async_remote_copy(
                 src_ref=sendb.at[s, 0],
                 dst_ref=pool.at[s, OWN + e, pl.ds(0, ROWS)],
                 send_sem=si_sem.at[s, m],
                 recv_sem=ri_sem.at[s, m],
-                device_id=at_elem(m),
+                device_id=at_elem(m) if m else sibling,
                 device_id_type=MESH,
             )
-        for r, o in enumerate(OFFSETS):
-            outer.append(
-                pltpu.make_async_remote_copy(
-                    src_ref=sendb.at[s, 1 + r // 2],
-                    dst_ref=pool.at[s, FAR + r, pl.ds(0, ROWS)],
-                    send_sem=sp_sem.at[s, r],
-                    recv_sem=rp_sem.at[s, r],
-                    device_id=at_dom(o),
-                    device_id_type=MESH,
-                )
+            for m in (*SAME_CORE, 0)
+        }
+
+    def relay(s, m):
+        copy = pltpu.make_async_remote_copy(
+            src_ref=pool.at[s, block_of(m), pl.ds(0, ROWS)],
+            dst_ref=pool.at[s, block_of(m), pl.ds(0, ROWS)],
+            send_sem=sr_sem.at[s, m],
+            recv_sem=rr_sem.at[s, m],
+            device_id=sibling,
+            device_id_type=MESH,
+        )
+        copy.start()
+        return copy
+
+    def relayed_block(m):
+        return OWN + (e + 1 - 2 * (e % 2) + N_ELEM - m) % N_ELEM
+
+    def start_halo(s):
+        own, inner, outer = own_copy(s), inner_copies(s), outer_copies(s)
+        inner[4].start()
+        outer[0].start()
+        outer[3].start()
+        inner[2].start()
+        inner[6].start()
+        outer[1].start()
+        outer[2].start()
+        inner[0].start()
+        own.start()
+        return own, inner, outer
+
+    def finish_halo(s, copies):
+        own, inner, outer = copies
+        relays = []
+        for m in (2, 6):
+            inner[m].wait_recv()
+            relays.append(relay(s, m))
+        own.wait()
+        inner[0].wait_recv()
+        other = OWN + e + 1 - 2 * (e % 2)
+        gather_pass(s, [OWN + e, other, block_of(2), block_of(6)], False)
+        inner[4].wait_recv()
+        relays.append(relay(s, 4))
+        for copy in outer:
+            copy.wait_recv()
+        gather_pass(s, [FAR, FAR + 1, FAR + 2, FAR + 3, block_of(4)], False)
+        for copy in relays:
+            copy.wait_recv()
+        gather_pass(s, [relayed_block(m) for m in (2, 6, 4)], False)
+        return [*inner.values(), *outer, *relays]
+
+    def outer_copies(s):
+        return [
+            pltpu.make_async_remote_copy(
+                src_ref=outb.at[s, r],
+                dst_ref=pool.at[s, FAR + r, pl.ds(0, 64)],
+                send_sem=sp_sem.at[s, r],
+                recv_sem=rp_sem.at[s, r],
+                device_id=at_dom(o),
+                device_id_type=MESH,
             )
-        for copy in [inner[4], outer[0], outer[3], inner[3], inner[5], outer[1], outer[2]]:
-            copy.start()
-        for m in (2, 6, 1, 7):
-            inner[m].start()
-        return own, inner, outer
+            for r, o in enumerate(OFFSETS)
+        ]
+
+    def own_copy(s):
+        return pltpu.make_async_copy(
+            sendb.at[s, 0], pool.at[s, OWN + e, pl.ds(0, ROWS)], own_sem.at[s]
+        )
 
     def component(s, chunk, c):
         return pool[s, chunk, pl.ds(c, 32, stride=4), :]
-
-    link_all = link[...]
-    near_link = jnp.where(link_all < 0, 0, link_all)
-    far = near_link >= 2560
-    lane_all = jnp.where(far, near_link - 2560, near_link) & 127
-    chunk_all = jnp.where(far, FAR + ((near_link - 2560) >> 6), near_link >> 7)
 
     def face_row(table, f, h):
         return table[f : f + 1, 128 * h : 128 * h + 128]
@@ -217,6 +323,18 @@
                 lane.append(rows_of(face_row(lane_all, f, h), 32))
                 chunk_of.append(rows_of(face_row(chunk_all, f, h), 32))
             for chunk in chunks:
+                if isinstance(chunk, int) and chunk >= FAR:
+                    p, u = (
+                        pool[s, chunk, pl.ds(c, 16, stride=4), :] for c in (0, 1 + f // 2)
+                    )
+                    values = p - sign * u
+                    for h in range(2):
+                        taken = jnp.concatenate(
+                            [lane_take(values, lane[h][0:16]), lane_take(values, lane[h][16:32] + 64)],
+                            axis=0,
+                        )
+                        kept[h] = jnp.where(chunk_of[h] == chunk, taken, kept[h])
+                    continue
                 values = component(s, chunk, 0) - sign * component(s, chunk, 1 + f // 2)
                 for h in range(2):
                     kept[h] = jnp.where(chunk_of[h] == chunk, lane_take(values, lane[h]), kept[h])
@@ -302,9 +420,6 @@
 
         lax.fori_loop(0, 5, step, 0, unroll=True)
 
-    patch = wpatch[...]
-    live = wface[...] >= 0
-
     def patch_tables():
         lane8, chunk8 = rows_of(patch & 127, 8), rows_of(patch >> 7, 8)
         lane32 = rows_of(patch & 127, 32)
@@ -334,7 +449,7 @@
             hit = jnp.where(face_column == lane + 128.0 * j, slot_column, 0.0)
             wslot[j] = rows_of(jnp.sum(hit, axis=0, keepdims=True), 32).astype(I32)
 
-    def walls(s, active, gain, rate):
+    def wall_terms(s, active):
         face_lane = rows_of(wface[...] & 127, 32)
         face_chunk = rows_of(wface[...] >> 7, 32)
         un = jnp.zeros((32, 128), F32)
@@ -344,82 +459,84 @@
                 taken = lane_take(component(s, 2 * f + h, 1 + f // 2), face_lane)
                 un = jnp.where(face_chunk == 2 * f + h, sign * taken, un)
         uslot[...] = un
+        weighted = weights[...] * uslot[pl.ds(0, 25), :]
+        for k in range(6):
+            fresh = jnp.sum(weighted * fwd[k, :, s, :].astype(F32), axis=0, keepdims=True)
+            fresh = (SECTION_B[s] * DT_STEP) * active[k : k + 1] * fresh
+            T[pl.ds(k, 1), :] = fresh if s == 0 else T[pl.ds(k, 1), :] + fresh
+
+    def wall_update(s, active, gain, rate):
         un = uslot[pl.ds(0, 25), :]
         value = jnp.zeros((25, 128), F32)
-        weighted = weights[...] * un
         aux_from, auxr_from = (aux_in, auxr_in) if s == 0 else (aux_out, auxr_out)
         for k in range(6):
             aux = aux_from[k]
             value = value + gain[k : k + 1] * aux
-            fresh = jnp.sum(weighted * fwd[k, :, s, :].astype(F32), axis=0, keepdims=True)
-            fresh = (SECTION_B[s] * DT_STEP) * active[k : k + 1] * fresh
-            T[pl.ds(k, 1), :] = fresh if s == 0 else T[pl.ds(k, 1), :] + fresh
             rate_k = active[k : k + 1] * (un - rate[k : k + 1] * aux)
             new = SECTION_A[s] * auxr_from[k] + DT_STEP * rate_k
             auxr_out[k] = new
             aux_out[k] = aux + SECTION_B[s] * new
         wall[pl.ds(0, 25), :] = value
 
-    def wait_halo(s, copies):
-        own, inner, outer = copies
-        own.wait()
-        for m in ELEM_ORDER:
-            inner[m].wait_recv()
-        for copy in outer:
-            copy.wait_recv()
-
-    def wait_sent(copies):
-        _, inner, outer = copies
-        for m in ELEM_ORDER:
-            inner[m].wait_send()
-        for copy in outer:
-            copy.wait_send()
-
-    load_a.wait()
-    make_traces(0)
+    sent_traces(0)
+    pack_outer(0)
     pl.semaphore_wait(barrier, len(partners))
-    copies = start_sends(0)
+    copies = start_halo(0)
+    own_traces(0)
+    loaded("wpatch", "wface", "link", "metric", "pcount", "amp", "decay")
+    link_all = link[...]
+    near_link = jnp.where(link_all < 0, 0, link_all)
+    far = near_link >= 2560
+    lane_all = jnp.where(far, (near_link - 2560) & 63, near_link & 127)
+    chunk_all = jnp.where(far, FAR + ((near_link - 2560) >> 6), near_link >> 7)
+
+    patch = wpatch[...]
+    live = wface[...] >= 0
     active, gain, rate = patch_tables()
     slot_tables()
+    loaded("weights", "aux", "auxr", "fwd", "dhigh", "dlow")
     T[...] = jnp.zeros((8, 128), F32)
     T[pl.ds(6, 1), :] = patch.astype(F32)
-    walls(0, active, gain, rate)
+    wall_terms(0, active)
+    wall_update(0, active, gain, rate)
     volume(0)
     gather_pass(0, range(OWN), True)
-    load_r.wait()
-    wait_halo(0, copies)
-    gather_pass(0, range(OWN, CHUNKS), False)
+    loaded("orient", "perm", "R")
+    sent = finish_halo(0, copies)
     fluxes(0)
     update(0)
 
-    make_traces(1)
-    copies_1 = start_sends(1)
-    walls(1, active, gain, rate)
-    Trecv[e] = T[...]
+    own_traces(1)
+    wall_terms(1, active)
     sums = []
-    for m in ELEM_ORDER:
+    for dx, m in PLANE:
         copy = pltpu.make_async_remote_copy(
             src_ref=T,
-            dst_ref=Trecv.at[e],
-            send_sem=sg_sem.at[m],
-            recv_sem=rg_sem.at[m],
-            device_id=at_elem(m),
+            dst_ref=Trecv.at[x * N_ELEM + e],
+            send_sem=sg_sem.at[dx, m],
+            recv_sem=rg_sem.at[dx, m],
+            device_id=at_xe(dx, m),
             device_id_type=MESH,
         )
         copy.start()
         sums.append(copy)
+    sent_traces(1)
+    pack_outer(1)
+    copies = start_halo(1)
+    Trecv[x * N_ELEM + e] = T[...]
+    wall_update(1, active, gain, rate)
     volume(1)
     gather_pass(1, range(OWN), True)
 
     for copy in sums:
         copy.wait_recv()
-    column = iota((512, 128), 0).astype(F32)
+    column = iota((128, 128), 0)
     highs, lows = [], []
-    for j in range(N_ELEM):
+    for j in range(NX * N_ELEM):
         ids = Trecv[j, pl.ds(6, 1), :].astype(I32)
-        at = ((ids >> 6) & 3) * 128 + (ids >> 8) * 8 + (ids & 7)
-        at = jnp.where(((ids >> 3) & 7) == e, at, -1).astype(F32)
-        onehot[:, pl.ds(128 * j, 128)] = jnp.where(column == rows_of(at, 512), 1.0, 0.0).astype(
+        at = (ids >> 8) * 8 + (ids & 7)
+        at = jnp.where(((ids >> 3) & 31) == (q % NX) * N_ELEM + e, at, -1)
+        onehot[:, pl.ds(128 * j, 128)] = jnp.where(column == rows_of(at, 128), 1.0, 0.0).astype(
             jnp.bfloat16
         )
         high, low = split(Trecv[j])
@@ -431,29 +548,7 @@
     binned = lax.dot_general(
         terms, onehot[...], (((1,), (1,)), ((), ())), preferred_element_type=F32
     )
-    binned = binned[0:8] + binned[8:16]
-    for j in range(NX):
-        X[j] = binned[:, 128 * j : 128 * j + 128]
-    Xrecv[x] = X[x]
-    sums_x = []
-    for m in range(1, NX):
-        copy = pltpu.make_async_remote_copy(
-            src_ref=X.at[(x + m) % NX],
-            dst_ref=Xrecv.at[x],
-            send_sem=sx_sem.at[m],
-            recv_sem=rx_sem.at[m],
-            device_id=at_x(m),
-            device_id_type=MESH,
-        )
-        copy.start()
-        sums_x.append(copy)
-
-    wait_halo(1, copies_1)
-    gather_pass(1, range(OWN, CHUNKS), False)
-
-    for copy in sums_x:
-        copy.wait_recv()
-    summed = Xrecv[0] + Xrecv[1] + Xrecv[2] + Xrecv[3]
+    summed = binned[0:8] + binned[8:16]
     lane16 = iota((8, 128), 1)
     for g in range(2):
         index = (8 * g + iota((8, 128), 0)) * 8 + (lane16 & 7)
@@ -478,12 +573,9 @@
         copy.start()
         sums_z.append(copy)
 
+    sent += finish_halo(1, copies)
     fluxes(1)
     update(1)
-    store_a = pltpu.make_async_copy(A, adj_out, load_sem.at[0])
-    store_r = pltpu.make_async_copy(R, reg_out, load_sem.at[1])
-    store_a.start()
-    store_r.start()
 
     for copy in sums_z:
         copy.wait_recv()
@@ -493,12 +585,20 @@
     index = (iota((8, 128), 0) + 8 * iota((8, 128), 1)) & 127
     grad_out[...] = lane_take(rows_of(row, 8), index)[:, 0:6]
 
-    wait_sent(copies)
-    wait_sent(copies_1)
-    for copy in sums + sums_x + sums_z:
+    for copy in sent + sums + sums_z:
         copy.wait_send()
-    store_a.wait()
-    store_r.wait()
+
+
+def store_kernel(*refs):
+    sources, targets, sem = refs[:5], refs[5:10], refs[10]
+    copies = [
+        pltpu.make_async_copy(source, target, sem.at[i])
+        for i, (source, target) in enumerate(zip(sources, targets))
+    ]
+    for copy in copies:
+        copy.start()
+    for copy in copies:
+        copy.wait()
 
 
 def body(
@@ -525,57 +625,9 @@
         return nodes.reshape(125, 2, 4, 128).transpose(2, 0, 1, 3).reshape(4, 125, 256)
 
     vmem = pl.BlockSpec(memory_space=pltpu.VMEM)
-    hbm = pl.BlockSpec(memory_space=pl.ANY)
+    hbm = pl.BlockSpec(memory_space=pltpu.HBM)
     dma = pltpu.SemaphoreType.DMA
-    adj, reg, aux, auxr, grad = pl.pallas_call(
-        kernel,
-        out_shape=[
-            jax.ShapeDtypeStruct((125, 8, 128), F32),
-            jax.ShapeDtypeStruct((125, 8, 128), F32),
-            jax.ShapeDtypeStruct((6, 25, 128), F32),
-            jax.ShapeDtypeStruct((6, 25, 128), F32),
-            jax.ShapeDtypeStruct((8, 6), F32),
-        ],
-        in_specs=[hbm, hbm] + [vmem] * 17,
-        out_specs=[hbm, hbm] + [vmem] * 3,
-        scratch_shapes=[
-            pltpu.VMEM((125, 8, 128), F32),
-            pltpu.VMEM((125, 8, 128), F32),
-            pltpu.VMEM((125, 8, 128), F32),
-            pltpu.VMEM((2, CHUNKS, 128, 128), F32),
-            pltpu.VMEM((2, 3, ROWS, 128), F32),
-            pltpu.VMEM((12, 32, 128), F32),
-            pltpu.VMEM((2, 32, 128), F32),
-            pltpu.VMEM((32, 128), F32),
-            pltpu.VMEM((12, 32, 128), I32),
-            pltpu.VMEM((32, 128), F32),
-            pltpu.VMEM((8, 128), F32),
-            pltpu.VMEM((8, 128), F32),
-            pltpu.VMEM((8, 128), F32),
-            pltpu.VMEM((N_ELEM, 8, 128), F32),
-            pltpu.VMEM((512, 1024), jnp.bfloat16),
-            pltpu.VMEM((NX, 8, 128), F32),
-            pltpu.VMEM((NX, 8, 128), F32),
-            pltpu.VMEM((NZ, 1, 128), F32),
-            pltpu.VMEM((NZ, 1, 128), F32),
-            dma((2,)),
-            dma((2,)),
-            dma((2, N_ELEM)),
-            dma((2, N_ELEM)),
-            dma((2, 4)),
-            dma((2, 4)),
-            dma((N_ELEM,)),
-            dma((N_ELEM,)),
-            dma((NX,)),
-            dma((NX,)),
-            dma((NZ,)),
-            dma((NZ,)),
-        ],
-        compiler_params=pltpu.CompilerParams(
-            collective_id=0, has_side_effects=True, vmem_limit_bytes=48 * 1024 * 1024
-        ),
-        cost_estimate=pl.CostEstimate(flops=400_000_000, bytes_accessed=3_000_000, transcendentals=0),
-    )(
+    operands = [
         packed(adjoint),
         packed(adjoint_reg),
         metric,
@@ -592,7 +644,80 @@
         wall_aux_reg,
         forward_aux.transpose(1, 2, 0, 3),
         *constant_tables(),
-    )
+    ]
+    outs = [
+        jax.ShapeDtypeStruct((125, 8, 128), F32),
+        jax.ShapeDtypeStruct((125, 8, 128), F32),
+        jax.ShapeDtypeStruct((6, 25, 128), F32),
+        jax.ShapeDtypeStruct((6, 25, 128), F32),
+        jax.ShapeDtypeStruct((8, 6), F32),
+    ]
+    results = pl.pallas_call(
+        kernel,
+        out_shape=outs,
+        in_specs=[hbm] * 19,
+        out_specs=[vmem] * 5,
+        scratch_shapes=[
+            pltpu.VMEM((3, 256), F32),
+            pltpu.VMEM((6, 256), I32),
+            pltpu.VMEM((6, 256), I32),
+            pltpu.VMEM((1, 128), I32),
+            pltpu.VMEM((4, 64), I32),
+            pltpu.VMEM((1, 128), I32),
+            pltpu.VMEM((1, 128), I32),
+            pltpu.VMEM((32, 128), I32),
+            pltpu.VMEM((6, 4096), F32),
+            pltpu.VMEM((6, 4096), F32),
+            pltpu.VMEM((6, 25, 128), F32),
+            pltpu.VMEM((6, 25, 128), F32),
+            pltpu.VMEM((6, 25, 2, 128), jnp.bfloat16),
+            pltpu.VMEM((384, 125), jnp.bfloat16),
+            pltpu.VMEM((384, 125), jnp.bfloat16),
+            pltpu.VMEM((256, 64), jnp.bfloat16),
+            pltpu.VMEM((25, 128), F32),
+            pltpu.VMEM((125, 8, 128), F32),
+            pltpu.VMEM((2, CHUNKS, 128, 128), F32),
+            pltpu.VMEM((2, 3, ROWS, 128), F32),
+            pltpu.VMEM((2, 4, 64, 128), F32),
+            pltpu.VMEM((12, 32, 128), F32),
+            pltpu.VMEM((2, 32, 128), F32),
+            pltpu.VMEM((32, 128), F32),
+            pltpu.VMEM((12, 32, 128), I32),
+            pltpu.VMEM((32, 128), F32),
+            pltpu.VMEM((8, 128), F32),
+            pltpu.VMEM((8, 128), F32),
+            pltpu.VMEM((8, 128), F32),
+            pltpu.VMEM((NX * N_ELEM, 8, 128), F32),
+            pltpu.VMEM((128, 4096), jnp.bfloat16),
+            pltpu.VMEM((NZ, 1, 128), F32),
+            pltpu.VMEM((NZ, 1, 128), F32),
+            dma((19,)),
+            dma((2,)),
+            dma((2, N_ELEM)),
+            dma((2, N_ELEM)),
+            dma((2, N_ELEM)),
+            dma((2, N_ELEM)),
+            dma((2, 4)),
+            dma((2, 4)),
+            dma((NX, N_ELEM)),
+            dma((NX, N_ELEM)),
+            dma((NZ,)),
+            dma((NZ,)),
+        ],
+        compiler_params=pltpu.CompilerParams(
+            collective_id=0, has_side_effects=True, vmem_limit_bytes=48 * 1024 * 1024
+        ),
+        cost_estimate=pl.CostEstimate(flops=400_000_000, bytes_accessed=3_000_000, transcendentals=0),
+    )(
+        *[pltpu.with_memory_space_constraint(value, pltpu.HBM) for value in operands]
+    )
+    adj, reg, aux, auxr, grad = pl.pallas_call(
+        store_kernel,
+        out_shape=outs,
+        in_specs=[vmem] * 5,
+        out_specs=[hbm] * 5,
+        scratch_shapes=[dma((5,))],
+    )(*[pltpu.with_memory_space_constraint(value, pltpu.VMEM) for value in results])
     return (unpacked(adj), unpacked(reg), aux, auxr, grad)
 
 

time: 62.6 us -> 40.8 us (0.65)
  the two profiles are of different devices: /device:TPU:1 before, /device:TPU:6 now
where the time goes in v2:
time: 40.8 us; the launch traced here: 40.6 us
  Pallas kernels  40 us (98%)
  between operations  0.65 us (2%)
    pallas_call x1, Pallas kernels, body(): pl.pallas_call(kernel, out_shape=outs, in_specs=[hbm] * 19, out_specs=[vm...  38.9 us
    pallas_call x1, Pallas kernels, body(): pl.pallas_call(store_kernel, out_shape=outs, in_specs=[vmem] * 5, out_spe...  1.05 us

profile of v2, /device:TPU:6, one launch (start us, length us, event | category | flops | bytes accessed | tf_op | source)
XLA Modules:
  0.0 40.6 jit_solution(9063455613048582850)
XLA Ops:
  0.6 38.9 %shard_map.218 = (f32[125,8,128]{2,1,0:T(8,128)S(1)}, f32[125,8,128]{2,1,0:T(8,128)S(1)}, f32[6,25,128]{2,1,0:T(8,128)S(1)}, f32[6,25,128]{2,1,0:T(8,128)S(1)}, f32[8,6]{1,0:T(8,128)S(1)}) custom-call(f32[125,8,128]{2,1,0:T(8,128)} %bitcast.27, f32[125,8,128]{2,1,0:T(8,128)} %bitcast.28, f32[3,256]{1,0:T(4,128)} %metric_hbm.1, s32[6,256]{1,0:T(8,128)} %link_hbm.1, ...), custom_call_target="tpu_custom_call" | custom-call | flops 400000000 | bytes 3000000 | tf_op jit(solution)/shard_map/pallas_call | solution.py:655
  39.6 1.0 %shard_map.219 = (f32[125,8,128]{2,1,0:T(8,128)}, f32[125,8,128]{2,1,0:T(8,128)}, f32[6,25,128]{2,1,0:T(8,128)}, f32[6,25,128]{2,1,0:T(8,128)}, f32[8,6]{1,0:T(8,128)}) custom-call(f32[125,8,128]{2,1,0:T(8,128)S(1)} %get-tuple-element.15.refs_0_, f32[125,8,128]{2,1,0:T(8,128)S(1)} %get-tuple-element.16.refs_1_, f32[6,25,128]{2,1,0:T(8,128)S(1)} %get-tuple-element.17.refs_2_, ...), custom_call_target="tpu_custom_call" | custom-call | tf_op jit(solution)/shard_map/pallas_call | solution.py:714

commit v3 on v2

--- a/solution.py
+++ b/solution.py
@@ -12,10 +12,12 @@
 SECTION_A = (-1.514183444257, -1.697784692471)
 SECTION_B = (0.1530572479681, 0.6994504559488)
 OFFSETS = (-2, -1, 1, 2)
+CROSS = (4,)
 SAME_CORE = (4, 2, 6)
 N_ELEM, N_DOM, NX, NZ = 8, 64, 4, 16
 OWN, FAR = 12, 20
 CHUNKS = 24
+FARTHEST_Z = (8, 7, 9, 6, 10, 5, 11, 4, 12, 3, 13, 2, 14, 1, 15)
 PLANE = tuple(
     sorted(
         ((dx, m) for dx in range(NX) for m in range(N_ELEM) if dx or m),
@@ -104,7 +106,7 @@
     A, R, aux_out, auxr_out, grad_out,
     metric, link, orient, isend, psend, wface, wpatch, pcount, amp, decay, aux_in, auxr_in, fwd,
     dhigh, dlow, perm, weights, S, pool, sendb, outb, G, lift, wall, wslot, uslot, ampb, decb, T, Trecv, onehot, Z, Zrecv,
-    load_sem, own_sem, si_sem, ri_sem, sr_sem, rr_sem, sp_sem, rp_sem, sg_sem, rg_sem, sz_sem, rz_sem,
+    load_sem, own_sem, si_sem, ri_sem, sc_sem, rc_sem, sr_sem, rr_sem, sp_sem, rp_sem, sg_sem, rg_sem, sz_sem, rz_sem,
 ):
     q = lax.axis_index("dom")
     e = lax.axis_index("elem")
@@ -147,18 +149,19 @@
         )
     ):
         loads[name] = pltpu.make_async_copy(source, target, load_sem.at[number])
+    barrier = pltpu.get_barrier_semaphore()
+
+    def greet(partners):
+        for partner in partners:
+            pl.semaphore_signal(barrier, inc=1, device_id=partner, device_id_type=MESH)
+
+    greet([at_z(m) for m in FARTHEST_Z])
     first = ("isend", "psend", "A")
     for name in first:
         loads[name].start()
-
-    partners = (
-        [at_xe(dx, m) for dx, m in PLANE]
-        + [at_dom(o) for o in OFFSETS]
-        + [at_z(m) for m in range(1, NZ)]
-    )
-    barrier = pltpu.get_barrier_semaphore()
-    for partner in partners:
-        pl.semaphore_signal(barrier, inc=1, device_id=partner, device_id_type=MESH)
+    greet([at_dom(o) for o in OFFSETS])
+    greet([at_xe(dx, m) for dx, m in PLANE])
+    greeted = NZ - 1 + len(OFFSETS) + len(PLANE)
     for name in loads:
         if name not in first:
             loads[name].start()
@@ -191,20 +194,20 @@
 
         lax.fori_loop(0, 5, one_row, 0)
 
-    def sent_traces(s):
+    def sent_traces(s, tables):
         lanes = [rows_of(row & 127, 8) for row in send_rows]
         faces = [rows_of(row >> 8, 8) for row in send_rows]
         halves = [rows_of((row >> 7) & 1, 4) == 1 for row in send_rows]
 
         def one_row(a, carry):
             for b in range(5):
-                kept = [jnp.zeros((8, 128), F32)] * 3
+                kept = {t: jnp.zeros((8, 128), F32) for t in tables}
                 for f in range(6):
                     n0, na, nb = FACE_NODE[f]
                     v = A[n0 + na * a + nb * b]
-                    for t in range(3):
+                    for t in tables:
                         kept[t] = jnp.where(faces[t] == f, lane_take(v, lanes[t]), kept[t])
-                for t in range(3):
+                for t in tables:
                     sendb[s, t, pl.ds(20 * a + 4 * b, 4), :] = jnp.where(
                         halves[t], kept[t][4:8], kept[t][0:4]
                     )
@@ -240,6 +243,19 @@
                 device_id_type=MESH,
             )
             for m in (*SAME_CORE, 0)
+        }
+
+    def cross_copies(s):
+        return {
+            m: pltpu.make_async_remote_copy(
+                src_ref=sendb.at[s, 0],
+                dst_ref=pool.at[s, OWN + e, pl.ds(0, ROWS)],
+                send_sem=sc_sem.at[s, m],
+                recv_sem=rc_sem.at[s, m],
+                device_id=(q, (e + m + 1 - 2 * (e % 2)) % N_ELEM),
+                device_id_type=MESH,
+            )
+            for m in CROSS
         }
 
     def relay(s, m):
@@ -258,37 +274,41 @@
         return OWN + (e + 1 - 2 * (e % 2) + N_ELEM - m) % N_ELEM
 
     def start_halo(s):
-        own, inner, outer = own_copy(s), inner_copies(s), outer_copies(s)
-        inner[4].start()
-        outer[0].start()
-        outer[3].start()
-        inner[2].start()
-        inner[6].start()
-        outer[1].start()
-        outer[2].start()
-        inner[0].start()
-        own.start()
-        return own, inner, outer
+        own, inner, cross, outer = own_copy(s), inner_copies(s), cross_copies(s), outer_copies(s)
+        sent_traces(s, (0,))
+        if s == 0:
+            pl.semaphore_wait(barrier, greeted)
+        for copy in (inner[4], cross[4], inner[2], inner[6], inner[0], own):
+            copy.start()
+        sent_traces(s, (1, 2))
+        pack_outer(s)
+        for r in (0, 3, 1, 2):
+            outer[r].start()
+        return own, inner, cross, outer
 
     def finish_halo(s, copies):
-        own, inner, outer = copies
+        own, inner, cross, outer = copies
         relays = []
-        for m in (2, 6):
+
+        def arrived(m):
             inner[m].wait_recv()
-            relays.append(relay(s, m))
+            if m not in cross:
+                relays.append(relay(s, m))
+
+        arrived(2)
+        arrived(6)
         own.wait()
         inner[0].wait_recv()
         other = OWN + e + 1 - 2 * (e % 2)
         gather_pass(s, [OWN + e, other, block_of(2), block_of(6)], False)
-        inner[4].wait_recv()
-        relays.append(relay(s, 4))
         for copy in outer:
             copy.wait_recv()
+        arrived(4)
         gather_pass(s, [FAR, FAR + 1, FAR + 2, FAR + 3, block_of(4)], False)
-        for copy in relays:
+        for copy in [*cross.values(), *relays]:
             copy.wait_recv()
         gather_pass(s, [relayed_block(m) for m in (2, 6, 4)], False)
-        return [*inner.values(), *outer, *relays]
+        return [*inner.values(), *cross.values(), *outer, *relays]
 
     def outer_copies(s):
         return [
@@ -478,9 +498,6 @@
             aux_out[k] = aux + SECTION_B[s] * new
         wall[pl.ds(0, 25), :] = value
 
-    sent_traces(0)
-    pack_outer(0)
-    pl.semaphore_wait(barrier, len(partners))
     copies = start_halo(0)
     own_traces(0)
     loaded("wpatch", "wface", "link", "metric", "pcount", "amp", "decay")
@@ -508,28 +525,23 @@
 
     own_traces(1)
     wall_terms(1, active)
-    sums = []
+    slot = x * N_ELEM + e
     for dx, m in PLANE:
-        copy = pltpu.make_async_remote_copy(
+        pltpu.make_async_remote_copy(
             src_ref=T,
-            dst_ref=Trecv.at[x * N_ELEM + e],
-            send_sem=sg_sem.at[dx, m],
-            recv_sem=rg_sem.at[dx, m],
+            dst_ref=Trecv.at[slot],
+            send_sem=sg_sem,
+            recv_sem=rg_sem,
             device_id=at_xe(dx, m),
             device_id_type=MESH,
-        )
-        copy.start()
-        sums.append(copy)
-    sent_traces(1)
-    pack_outer(1)
+        ).start()
+    pltpu.make_async_copy(T, Trecv.at[slot], rg_sem).start()
     copies = start_halo(1)
-    Trecv[x * N_ELEM + e] = T[...]
     wall_update(1, active, gain, rate)
     volume(1)
     gather_pass(1, range(OWN), True)
 
-    for copy in sums:
-        copy.wait_recv()
+    pltpu.make_async_copy(Trecv, Trecv, rg_sem).wait()
     column = iota((128, 128), 0)
     highs, lows = [], []
     for j in range(NX * N_ELEM):
@@ -559,34 +571,33 @@
             )
         for i in range(8):
             Z[8 * g + i] = block[i : i + 1]
-    Zrecv[z] = Z[z]
-    sums_z = []
-    for m in range(1, NZ):
-        copy = pltpu.make_async_remote_copy(
+    for m in FARTHEST_Z:
+        pltpu.make_async_remote_copy(
             src_ref=Z.at[(z + m) % NZ],
             dst_ref=Zrecv.at[z],
-            send_sem=sz_sem.at[m],
-            recv_sem=rz_sem.at[m],
+            send_sem=sz_sem,
+            recv_sem=rz_sem,
             device_id=at_z(m),
             device_id_type=MESH,
-        )
-        copy.start()
-        sums_z.append(copy)
+        ).start()
+    pltpu.make_async_copy(Z.at[z], Zrecv.at[z], rz_sem).start()
 
     sent += finish_halo(1, copies)
     fluxes(1)
     update(1)
 
-    for copy in sums_z:
-        copy.wait_recv()
+    for copy in sent:
+        copy.wait_send()
+    most = pl.ds(0, NX * N_ELEM - 1)
+    pltpu.make_async_copy(Trecv.at[most], Trecv.at[most], sg_sem).wait()
+    most = pl.ds(0, NZ - 1)
+    pltpu.make_async_copy(Z.at[most], Z.at[most], sz_sem).wait()
+    pltpu.make_async_copy(Zrecv, Zrecv, rz_sem).wait()
     row = Zrecv[0]
     for j in range(1, NZ):
         row = row + Zrecv[j]
     index = (iota((8, 128), 0) + 8 * iota((8, 128), 1)) & 127
     grad_out[...] = lane_take(rows_of(row, 8), index)[:, 0:6]
-
-    for copy in sent + sums + sums_z:
-        copy.wait_send()
 
 
 def store_kernel(*refs):
@@ -697,12 +708,14 @@
             dma((2, N_ELEM)),
             dma((2, N_ELEM)),
             dma((2, N_ELEM)),
+            dma((2, N_ELEM)),
+            dma((2, N_ELEM)),
             dma((2, 4)),
             dma((2, 4)),
-            dma((NX, N_ELEM)),
-            dma((NX, N_ELEM)),
-            dma((NZ,)),
-            dma((NZ,)),
+            dma,
+            dma,
+            dma,
+            dma,
         ],
         compiler_params=pltpu.CompilerParams(
             collective_id=0, has_side_effects=True, vmem_limit_bytes=48 * 1024 * 1024

time: 40.8 us -> 39.9 us (0.978)
  the two profiles are of different devices: /device:TPU:6 before, /device:TPU:1 now
where the time goes in v3:
time: 39.9 us; the launch traced here: 39.7 us
  Pallas kernels  39.1 us (98%)
  between operations  0.65 us (2%)
    pallas_call x1, Pallas kernels, body(): pl.pallas_call(kernel, out_shape=outs, in_specs=[hbm] * 19, out_specs=[vm...  38 us
    pallas_call x1, Pallas kernels, body(): pl.pallas_call(store_kernel, out_shape=outs, in_specs=[vmem] * 5, out_spe...  1.05 us

profile of v3, /device:TPU:1, one launch (start us, length us, event | category | flops | bytes accessed | tf_op | source)
XLA Modules:
  0.0 39.7 jit_solution(7866199600212656958)
XLA Ops:
  0.6 38.0 %shard_map.218 = (f32[125,8,128]{2,1,0:T(8,128)S(1)}, f32[125,8,128]{2,1,0:T(8,128)S(1)}, f32[6,25,128]{2,1,0:T(8,128)S(1)}, f32[6,25,128]{2,1,0:T(8,128)S(1)}, f32[8,6]{1,0:T(8,128)S(1)}) custom-call(f32[125,8,128]{2,1,0:T(8,128)} %bitcast.27, f32[125,8,128]{2,1,0:T(8,128)} %bitcast.28, f32[3,256]{1,0:T(4,128)} %metric_hbm.1, s32[6,256]{1,0:T(8,128)} %link_hbm.1, ...), custom_call_target="tpu_custom_call" | custom-call | flops 400000000 | bytes 3000000 | tf_op jit(solution)/shard_map/pallas_call | solution.py:666
  38.7 1.0 %shard_map.219 = (f32[125,8,128]{2,1,0:T(8,128)}, f32[125,8,128]{2,1,0:T(8,128)}, f32[6,25,128]{2,1,0:T(8,128)}, f32[6,25,128]{2,1,0:T(8,128)}, f32[8,6]{1,0:T(8,128)}) custom-call(f32[125,8,128]{2,1,0:T(8,128)S(1)} %get-tuple-element.15.refs_0_, f32[125,8,128]{2,1,0:T(8,128)S(1)} %get-tuple-element.16.refs_1_, f32[6,25,128]{2,1,0:T(8,128)S(1)} %get-tuple-element.17.refs_2_, ...), custom_call_target="tpu_custom_call" | custom-call | tf_op jit(solution)/shard_map/pallas_call | solution.py:727

commit v4 on v3

--- a/solution.py
+++ b/solution.py
@@ -106,7 +106,7 @@
     A, R, aux_out, auxr_out, grad_out,
     metric, link, orient, isend, psend, wface, wpatch, pcount, amp, decay, aux_in, auxr_in, fwd,
     dhigh, dlow, perm, weights, S, pool, sendb, outb, G, lift, wall, wslot, uslot, ampb, decb, T, Trecv, onehot, Z, Zrecv,
-    load_sem, own_sem, si_sem, ri_sem, sc_sem, rc_sem, sr_sem, rr_sem, sp_sem, rp_sem, sg_sem, rg_sem, sz_sem, rz_sem,
+    load_sem, own_sem, si_sem, ri_sem, sc_sem, rc_sem, sr_sem, rr_sem, sp_sem, rp_sem, sg_sem, rg_sem, sz_sem, rz_sem, known_sem,
 ):
     q = lax.axis_index("dom")
     e = lax.axis_index("elem")
@@ -155,13 +155,20 @@
         for partner in partners:
             pl.semaphore_signal(barrier, inc=1, device_id=partner, device_id_type=MESH)
 
-    greet([at_z(m) for m in FARTHEST_Z])
     first = ("isend", "psend", "A")
     for name in first:
         loads[name].start()
-    greet([at_dom(o) for o in OFFSETS])
-    greet([at_xe(dx, m) for dx, m in PLANE])
-    greeted = NZ - 1 + len(OFFSETS) + len(PLANE)
+    greet([at_dom(o) for o in (-4, 4, -3, 3, -2, 2, -1, 1)])
+    greet([at_elem(m) for m in range(1, N_ELEM)])
+    greeted = 8 + N_ELEM - 1
+
+    def vouch(step):
+        for m in (2**step, NZ - 2**step):
+            pl.semaphore_signal(known_sem.at[step], inc=1, device_id=at_z(m), device_id_type=MESH)
+
+    def vouched(step):
+        pl.semaphore_wait(known_sem.at[step], 2)
+
     for name in loads:
         if name not in first:
             loads[name].start()
@@ -278,6 +285,7 @@
         sent_traces(s, (0,))
         if s == 0:
             pl.semaphore_wait(barrier, greeted)
+            vouch(0)
         for copy in (inner[4], cross[4], inner[2], inner[6], inner[0], own):
             copy.start()
         sent_traces(s, (1, 2))
@@ -519,6 +527,8 @@
     volume(0)
     gather_pass(0, range(OWN), True)
     loaded("orient", "perm", "R")
+    vouched(0)
+    vouch(1)
     sent = finish_halo(0, copies)
     fluxes(0)
     update(0)
@@ -536,6 +546,8 @@
             device_id_type=MESH,
         ).start()
     pltpu.make_async_copy(T, Trecv.at[slot], rg_sem).start()
+    vouched(1)
+    vouch(2)
     copies = start_halo(1)
     wall_update(1, active, gain, rate)
     volume(1)
@@ -571,6 +583,7 @@
             )
         for i in range(8):
             Z[8 * g + i] = block[i : i + 1]
+    vouched(2)
     for m in FARTHEST_Z:
         pltpu.make_async_remote_copy(
             src_ref=Z.at[(z + m) % NZ],
@@ -716,6 +729,7 @@
             dma,
             dma,
             dma,
+            pltpu.SemaphoreType.REGULAR((3,)),
         ],
         compiler_params=pltpu.CompilerParams(
             collective_id=0, has_side_effects=True, vmem_limit_bytes=48 * 1024 * 1024

time: 39.9 us -> 37.9 us (0.950)
  Pallas kernels: 39.1 us -> 37.1 us
    pallas_call x1, Pallas kernels: 38 us -> 36 us  [body(): pl.pallas_call(kernel, out_shape=outs, in_specs=[hbm] * 19, out_specs=[vm...]
where the time goes in v4:
time: 37.9 us; the launch traced here: 37.7 us
  Pallas kernels  37.1 us (98%)
  between operations  0.65 us (2%)
    pallas_call x1, Pallas kernels, body(): pl.pallas_call(kernel, out_shape=outs, in_specs=[hbm] * 19, out_specs=[vm...  36 us
    pallas_call x1, Pallas kernels, body(): pl.pallas_call(store_kernel, out_shape=outs, in_specs=[vmem] * 5, out_spe...  1.05 us

profile of v4, /device:TPU:1, one launch (start us, length us, event | category | flops | bytes accessed | tf_op | source)
XLA Modules:
  0.0 37.7 jit_solution(3704294895124236556)
XLA Ops:
  0.6 36.0 %shard_map.218 = (f32[125,8,128]{2,1,0:T(8,128)S(1)}, f32[125,8,128]{2,1,0:T(8,128)S(1)}, f32[6,25,128]{2,1,0:T(8,128)S(1)}, f32[6,25,128]{2,1,0:T(8,128)S(1)}, f32[8,6]{1,0:T(8,128)S(1)}) custom-call(f32[125,8,128]{2,1,0:T(8,128)} %bitcast.27, f32[125,8,128]{2,1,0:T(8,128)} %bitcast.28, f32[3,256]{1,0:T(4,128)} %metric_hbm.1, s32[6,256]{1,0:T(8,128)} %link_hbm.1, ...), custom_call_target="tpu_custom_call" | custom-call | flops 400000000 | bytes 3000000 | tf_op jit(solution)/shard_map/pallas_call | solution.py:679
  36.7 1.0 %shard_map.219 = (f32[125,8,128]{2,1,0:T(8,128)}, f32[125,8,128]{2,1,0:T(8,128)}, f32[6,25,128]{2,1,0:T(8,128)}, f32[6,25,128]{2,1,0:T(8,128)}, f32[8,6]{1,0:T(8,128)}) custom-call(f32[125,8,128]{2,1,0:T(8,128)S(1)} %get-tuple-element.15.refs_0_, f32[125,8,128]{2,1,0:T(8,128)S(1)} %get-tuple-element.16.refs_1_, f32[6,25,128]{2,1,0:T(8,128)S(1)} %get-tuple-element.17.refs_2_, ...), custom_call_target="tpu_custom_call" | custom-call | tf_op jit(solution)/shard_map/pallas_call | solution.py:741

commit v5 on v4

--- a/solution.py
+++ b/solution.py
@@ -12,7 +12,7 @@
 SECTION_A = (-1.514183444257, -1.697784692471)
 SECTION_B = (0.1530572479681, 0.6994504559488)
 OFFSETS = (-2, -1, 1, 2)
-CROSS = (4,)
+CROSS = (4, 2, 6)
 SAME_CORE = (4, 2, 6)
 N_ELEM, N_DOM, NX, NZ = 8, 64, 4, 16
 OWN, FAR = 12, 20
@@ -286,7 +286,7 @@
         if s == 0:
             pl.semaphore_wait(barrier, greeted)
             vouch(0)
-        for copy in (inner[4], cross[4], inner[2], inner[6], inner[0], own):
+        for copy in (inner[4], cross[4], inner[2], inner[6], cross[2], cross[6], inner[0], own):
             copy.start()
         sent_traces(s, (1, 2))
         pack_outer(s)
@@ -484,7 +484,14 @@
         for f in range(6):
             sign = -1.0 if f % 2 == 0 else 1.0
             for h in range(2):
-                taken = lane_take(component(s, 2 * f + h, 1 + f // 2), face_lane)
+                n0, _, nb = FACE_NODE[f]
+                base = 8 * n0 + 4 * h + 1 + f // 2
+                if f // 2 != 1:
+                    G[2 * f + h, pl.ds(0, 25), :] = A2[pl.ds(base, 25, stride=8 * nb), :]
+                else:
+                    for a in range(5):
+                        G[2 * f + h, pl.ds(5 * a, 5), :] = A2[pl.ds(base + 200 * a, 5, stride=8), :]
+                taken = lane_take(G[2 * f + h], face_lane)
                 un = jnp.where(face_chunk == 2 * f + h, sign * taken, un)
         uslot[...] = un
         weighted = weights[...] * uslot[pl.ds(0, 25), :]
@@ -533,7 +540,6 @@
     fluxes(0)
     update(0)
 
-    own_traces(1)
     wall_terms(1, active)
     slot = x * N_ELEM + e
     for dx, m in PLANE:
@@ -549,6 +555,7 @@
     vouched(1)
     vouch(2)
     copies = start_halo(1)
+    own_traces(1)
     wall_update(1, active, gain, rate)
     volume(1)
     gather_pass(1, range(OWN), True)

time: 37.9 us -> 37.6 us (level)
  no operation moved by 1% of the time
where the time goes in v5:
time: 37.6 us; the launch traced here: 37.4 us
  Pallas kernels  36.8 us (98%)
  between operations  0.65 us (2%)
    pallas_call x1, Pallas kernels, body(): pl.pallas_call(kernel, out_shape=outs, in_specs=[hbm] * 19, out_specs=[vm...  35.7 us
    pallas_call x1, Pallas kernels, body(): pl.pallas_call(store_kernel, out_shape=outs, in_specs=[vmem] * 5, out_spe...  1.05 us

profile of v5, /device:TPU:1, one launch (start us, length us, event | category | flops | bytes accessed | tf_op | source)
XLA Modules:
  0.0 37.4 jit_solution(4501490932337042236)
XLA Ops:
  0.6 35.7 %shard_map.218 = (f32[125,8,128]{2,1,0:T(8,128)S(1)}, f32[125,8,128]{2,1,0:T(8,128)S(1)}, f32[6,25,128]{2,1,0:T(8,128)S(1)}, f32[6,25,128]{2,1,0:T(8,128)S(1)}, f32[8,6]{1,0:T(8,128)S(1)}) custom-call(f32[125,8,128]{2,1,0:T(8,128)} %bitcast.27, f32[125,8,128]{2,1,0:T(8,128)} %bitcast.28, f32[3,256]{1,0:T(4,128)} %metric_hbm.1, s32[6,256]{1,0:T(8,128)} %link_hbm.1, ...), custom_call_target="tpu_custom_call" | custom-call | flops 400000000 | bytes 3000000 | tf_op jit(solution)/shard_map/pallas_call | solution.py:686
  36.4 1.0 %shard_map.219 = (f32[125,8,128]{2,1,0:T(8,128)}, f32[125,8,128]{2,1,0:T(8,128)}, f32[6,25,128]{2,1,0:T(8,128)}, f32[6,25,128]{2,1,0:T(8,128)}, f32[8,6]{1,0:T(8,128)}) custom-call(f32[125,8,128]{2,1,0:T(8,128)S(1)} %get-tuple-element.15.refs_0_, f32[125,8,128]{2,1,0:T(8,128)S(1)} %get-tuple-element.16.refs_1_, f32[6,25,128]{2,1,0:T(8,128)S(1)} %get-tuple-element.17.refs_2_, ...), custom_call_target="tpu_custom_call" | custom-call | tf_op jit(solution)/shard_map/pallas_call | solution.py:748
